TPU v7x, 512 devices: a whole 4x8x8 slice. The times are simulated.
512 devices in a mesh: dp: 16 (over y, x_lo), query: 32 (over x_hi, z, core).
Axes of the slice: x: 4 (x_hi: 2, x_lo: 2; x = x_hi * 2 + x_lo), y: 8, z: 8, core: 2. Of those that a mesh axis runs over, the one named last changes fastest.
Arguments:
- activations: bfloat16 [65536, 14336], P(('dp', 'query')), may hold values from -200 to 200, as said below
- out_grads: bfloat16 [65536, 4096], P(('dp', 'query')), may hold values from -200 to 200, as said below
- in_projection: bfloat16 [64, 14336], P(None, 'query'), may hold values from -1 to 1
- out_projection: bfloat16 [64, 4096], P(None, 'query'), may hold values from -1 to 1
- lengths: int32 [4096], P(('dp', 'query')), may hold values from 1 to 16, 49152 in all
- queries: bfloat16 [1024, 4096], P('query'), may hold values from -0.09375 to 0.09375
Outputs:
- scores: float32 [4096, 1024], P(('dp', 'query'))
Inputs may be any that keep to these rules, and one draw needn't show every extreme that they name: activations are finite with magnitudes below 200. out_grads are finite with magnitudes below 200. `lengths`: some example has all 16 slots live.
All inputs are finite; a program needn't handle non-finite values. No bound on the sum of `lengths` on one device may be relied on, other than what follows from the above.
Results may differ from a plain program's by a relative error of at most 0.0003.
Values may be sent and summed in bfloat16 or wider, within the bound.
A program may use at most 64 MiB of HBM per device.

v0:
```python
import jax
import jax.numpy as jnp
from jax import lax
from jax.sharding import PartitionSpec as P


def passed_along(value, axis, steps):
    count = lax.axis_size(axis)
    pairs = [(source, (source + steps) % count) for source in range(count)]
    return lax.ppermute(value, axis, pairs)


def damped_inverse(factor):
    rank_size = factor.shape[0]
    identity = jnp.eye(rank_size, dtype=jnp.float32)
    damped = factor + 0.1 * jnp.trace(factor) / rank_size * identity
    lower_factor = jnp.linalg.cholesky(damped)
    lower_inverse = lax.linalg.triangular_solve(lower_factor, identity, left_side=True, lower=True)
    return jnp.dot(lower_inverse.T, lower_inverse, precision=lax.Precision.HIGHEST)


def fold_columns(source, segment):
    return lax.dot_general(
        source, segment, (((1,), (1,)), ((), ())), preferred_element_type=jnp.float32
    )


def score_block(preconditioned, query_block):
    return lax.dot_general(
        preconditioned,
        query_block.astype(jnp.float32),
        (((1,), (1,)), ((), ())),
        precision=lax.Precision.HIGHEST,
    )


def on_device(activations, out_grads, in_projection, out_projection, lengths, queries):
    tok_rows = activations.shape[0]
    rank_size = in_projection.shape[0]
    examples_here = lengths.shape[0]
    seq_len = tok_rows // examples_here
    cycle_size = lax.axis_size("query")
    my_index = lax.axis_index("query")
    block_rows = queries.shape[0]
    tokens_all = tok_rows * lax.axis_size("dp") * cycle_size
    projected_in = fold_columns(
        activations, lax.all_gather(in_projection, "query", axis=1, tiled=True)
    )
    projected_out = fold_columns(
        out_grads, lax.all_gather(out_projection, "query", axis=1, tiled=True)
    )
    positions = jnp.arange(seq_len, dtype=jnp.int32)
    live = (positions[None, :] < lengths[:, None]).astype(jnp.float32).reshape(tok_rows, 1)
    masked_in = projected_in * live
    masked_out = projected_out * live
    in_partial = jnp.dot(masked_in.T, projected_in, precision=lax.Precision.HIGHEST)
    out_partial = jnp.dot(masked_out.T, projected_out, precision=lax.Precision.HIGHEST)
    factors = lax.psum(jnp.stack([in_partial, out_partial]), ("dp", "query")) / tokens_all
    in_inverse = damped_inverse(factors[0])
    out_inverse = damped_inverse(factors[1])
    example_grads = jnp.einsum(
        "esi,esj->eij",
        masked_out.reshape(examples_here, seq_len, rank_size),
        projected_in.reshape(examples_here, seq_len, rank_size),
        precision=lax.Precision.HIGHEST,
    )
    left_done = jnp.einsum(
        "ik,ekj->eij", out_inverse, example_grads, precision=lax.Precision.HIGHEST
    )
    preconditioned = jnp.einsum(
        "eik,kj->eij", left_done, in_inverse, precision=lax.Precision.HIGHEST
    )
    preconditioned = preconditioned.reshape(examples_here, rank_size * rank_size)

    def cycle_turn(turn, state_pair):
        query_block, gathered = state_pair
        source = (my_index - turn) % cycle_size
        gathered = lax.dynamic_update_slice(
            gathered, score_block(preconditioned, query_block), (jnp.int32(0), source * block_rows)
        )
        query_block = passed_along(query_block, "query", 1)
        return (query_block, gathered)

    start_scores = jnp.zeros((examples_here, cycle_size * block_rows), jnp.float32)
    last_block, gathered = lax.fori_loop(0, cycle_size - 1, cycle_turn, (queries, start_scores))
    source = (my_index - (cycle_size - 1)) % cycle_size
    scores = lax.dynamic_update_slice(
        gathered, score_block(preconditioned, last_block), (jnp.int32(0), source * block_rows)
    )
    return scores


def solution(mesh):
    placed = (
        P(("dp", "query"), None),
        P(("dp", "query"), None),
        P(None, "query"),
        P(None, "query"),
        P(("dp", "query")),
        P("query", None),
    )
    return jax.shard_map(
        on_device, mesh=mesh, in_specs=placed, out_specs=P(("dp", "query"), None), check_vma=False
    )
```

profile of v0, /device:TPU:1, one launch (start us, length us, event | category | flops | bytes accessed | tf_op | source)
XLA Modules:
  0.0 590.6 jit_solution(6379022868898756825)
XLA Ops:
  8.1 51.1 %all_gather.6 = bf16[64,4096]{1,0:T(8,128)(2,1)S(1)} all-gather(bf16[64,128]{1,0:T(8,128)(2,1)} %param.14), channel_id=1, replica_groups=mesh['dp'=16,'query'=32] {'query'}, dimensions={1}, use_global_device_ids=true | all-gather | bytes 540672 | tf_op jit(solution)/shard_map/all_gather | solution.py:50
  60.0 42.8 %all-gather.3.cloned.1.call-done = bf16[32,448,64]{1,2,0:T(8,128)(2,1)} async-done(((bf16[1,448,64]{1,2,0:T(8,128)(2,1)}), bf16[32,448,64]{1,2,0:T(8,128)(2,1)}) %all-gather.3.cloned.1.call-update) | async-done | bytes 1835024 | tf_op jit(solution)/shard_map/all_gather | solution.py:47
  102.8 2.8 copy.19
  105.5 3.4 reshape.46
  108.9 4.0 fusion.14
  113.2 95.8 %psum.7 = f32[2,64,64]{1,2,0:T(8,128)S(1)} all-reduce(f32[2,64,64]{1,2,0:T(8,128)S(1)} %pad_maximum_fusion), channel_id=1, replica_groups=mesh['dp'=16,'query'=32] {'dp','query'}, use_global_device_ids=true, to_apply=%region_0.0 | all-reduce | flops 8192 | bytes 65536 | tf_op jit(solution)/shard_map/psum | solution.py:58
  211.1 5.8 cholesky.55
  218.4 4.9 custom-call.7
  223.8 5.8 cholesky.44
  231.1 4.9 custom-call.6
  238.3 343.5 %while.17 = (s32[]{:T(128)}, bf16[32,4096]{1,0:T(8,128)(2,1)S(1)}, f32[8,1024]{1,0:T(8,128)S(1)}, f32[8,4096]{1,0:T(8,128)S(1)}, s32[]{:T(128)}, /*index=5*/s32[...) while((s32[]{:T(128)}, bf16[32,4096]{1,0:T(8,128)(2,1)S(1)}, f32[8,1024]{1,0:T(8,128)S(1)}, ...), condition=%wide.region_6.9_spmd, body=%wide.region_5.8_spmd.sunk | while | flops 12582930 | bytes 1969464 | solution.py:85
  238.3 2.8 collective-permute-start
  241.6 2.8 collective-permute-done
  244.4 4.4 collective-permute-start
  249.3 4.0 collective-permute-done
  253.3 3.2 collective-permute-start
  257.0 7.6 %collective-permute-done = bf16[32,4096]{1,0:T(8,128)(2,1)S(1)} collective-permute-done((bf16[32,4096]{1,0:T(8,128)(2,1)S(1)}, bf16[32,4096]{1,0:T(8,128)(2,1)S(1)}, u32[]{:S(2)}, u32[]{:S(2)}) %collective-permute-start) | collective-permute-done | bytes 262176 | tf_op jit(solution)/shard_map/while/body/eval_jaxpr/ppermute | solution.py:10
  264.6 1.9 collective-permute-start
  267.0 8.9 %collective-permute-done = bf16[32,4096]{1,0:T(8,128)(2,1)S(1)} collective-permute-done((bf16[32,4096]{1,0:T(8,128)(2,1)S(1)}, bf16[32,4096]{1,0:T(8,128)(2,1)S(1)}, u32[]{:S(2)}, u32[]{:S(2)}) %collective-permute-start) | collective-permute-done | bytes 262176 | tf_op jit(solution)/shard_map/while/body/eval_jaxpr/ppermute | solution.py:10
  275.9 1.9 collective-permute-start
  278.3 8.9 %collective-permute-done = bf16[32,4096]{1,0:T(8,128)(2,1)S(1)} collective-permute-done((bf16[32,4096]{1,0:T(8,128)(2,1)S(1)}, bf16[32,4096]{1,0:T(8,128)(2,1)S(1)}, u32[]{:S(2)}, u32[]{:S(2)}) %collective-permute-start) | collective-permute-done | bytes 262176 | tf_op jit(solution)/shard_map/while/body/eval_jaxpr/ppermute | solution.py:10
  287.2 1.9 collective-permute-start
  289.6 8.9 %collective-permute-done = bf16[32,4096]{1,0:T(8,128)(2,1)S(1)} collective-permute-done((bf16[32,4096]{1,0:T(8,128)(2,1)S(1)}, bf16[32,4096]{1,0:T(8,128)(2,1)S(1)}, u32[]{:S(2)}, u32[]{:S(2)}) %collective-permute-start) | collective-permute-done | bytes 262176 | tf_op jit(solution)/shard_map/while/body/eval_jaxpr/ppermute | solution.py:10
  298.6 1.9 collective-permute-start
  301.0 8.8 %collective-permute-done = bf16[32,4096]{1,0:T(8,128)(2,1)S(1)} collective-permute-done((bf16[32,4096]{1,0:T(8,128)(2,1)S(1)}, bf16[32,4096]{1,0:T(8,128)(2,1)S(1)}, u32[]{:S(2)}, u32[]{:S(2)}) %collective-permute-start) | collective-permute-done | bytes 262176 | tf_op jit(solution)/shard_map/while/body/eval_jaxpr/ppermute | solution.py:10
  309.9 1.9 collective-permute-start
  312.4 8.8 %collective-permute-done = bf16[32,4096]{1,0:T(8,128)(2,1)S(1)} collective-permute-done((bf16[32,4096]{1,0:T(8,128)(2,1)S(1)}, bf16[32,4096]{1,0:T(8,128)(2,1)S(1)}, u32[]{:S(2)}, u32[]{:S(2)}) %collective-permute-start) | collective-permute-done | bytes 262176 | tf_op jit(solution)/shard_map/while/body/eval_jaxpr/ppermute | solution.py:10
  321.2 1.9 collective-permute-start
  323.7 8.8 %collective-permute-done = bf16[32,4096]{1,0:T(8,128)(2,1)S(1)} collective-permute-done((bf16[32,4096]{1,0:T(8,128)(2,1)S(1)}, bf16[32,4096]{1,0:T(8,128)(2,1)S(1)}, u32[]{:S(2)}, u32[]{:S(2)}) %collective-permute-start) | collective-permute-done | bytes 262176 | tf_op jit(solution)/shard_map/while/body/eval_jaxpr/ppermute | solution.py:10
  332.5 1.9 collective-permute-start
  335.0 8.9 %collective-permute-done = bf16[32,4096]{1,0:T(8,128)(2,1)S(1)} collective-permute-done((bf16[32,4096]{1,0:T(8,128)(2,1)S(1)}, bf16[32,4096]{1,0:T(8,128)(2,1)S(1)}, u32[]{:S(2)}, u32[]{:S(2)}) %collective-permute-start) | collective-permute-done | bytes 262176 | tf_op jit(solution)/shard_map/while/body/eval_jaxpr/ppermute | solution.py:10
  343.9 1.9 collective-permute-start
  346.3 8.8 %collective-permute-done = bf16[32,4096]{1,0:T(8,128)(2,1)S(1)} collective-permute-done((bf16[32,4096]{1,0:T(8,128)(2,1)S(1)}, bf16[32,4096]{1,0:T(8,128)(2,1)S(1)}, u32[]{:S(2)}, u32[]{:S(2)}) %collective-permute-start) | collective-permute-done | bytes 262176 | tf_op jit(solution)/shard_map/while/body/eval_jaxpr/ppermute | solution.py:10
  355.2 1.9 collective-permute-start
  357.7 8.8 %collective-permute-done = bf16[32,4096]{1,0:T(8,128)(2,1)S(1)} collective-permute-done((bf16[32,4096]{1,0:T(8,128)(2,1)S(1)}, bf16[32,4096]{1,0:T(8,128)(2,1)S(1)}, u32[]{:S(2)}, u32[]{:S(2)}) %collective-permute-start) | collective-permute-done | bytes 262176 | tf_op jit(solution)/shard_map/while/body/eval_jaxpr/ppermute | solution.py:10
  366.5 1.9 collective-permute-start
  369.0 8.8 %collective-permute-done = bf16[32,4096]{1,0:T(8,128)(2,1)S(1)} collective-permute-done((bf16[32,4096]{1,0:T(8,128)(2,1)S(1)}, bf16[32,4096]{1,0:T(8,128)(2,1)S(1)}, u32[]{:S(2)}, u32[]{:S(2)}) %collective-permute-start) | collective-permute-done | bytes 262176 | tf_op jit(solution)/shard_map/while/body/eval_jaxpr/ppermute | solution.py:10
  377.8 1.9 collective-permute-start
  380.3 8.9 %collective-permute-done = bf16[32,4096]{1,0:T(8,128)(2,1)S(1)} collective-permute-done((bf16[32,4096]{1,0:T(8,128)(2,1)S(1)}, bf16[32,4096]{1,0:T(8,128)(2,1)S(1)}, u32[]{:S(2)}, u32[]{:S(2)}) %collective-permute-start) | collective-permute-done | bytes 262176 | tf_op jit(solution)/shard_map/while/body/eval_jaxpr/ppermute | solution.py:10
  389.2 1.9 collective-permute-start
  391.6 8.8 %collective-permute-done = bf16[32,4096]{1,0:T(8,128)(2,1)S(1)} collective-permute-done((bf16[32,4096]{1,0:T(8,128)(2,1)S(1)}, bf16[32,4096]{1,0:T(8,128)(2,1)S(1)}, u32[]{:S(2)}, u32[]{:S(2)}) %collective-permute-start) | collective-permute-done | bytes 262176 | tf_op jit(solution)/shard_map/while/body/eval_jaxpr/ppermute | solution.py:10
  400.5 1.9 collective-permute-start
  403.0 8.8 %collective-permute-done = bf16[32,4096]{1,0:T(8,128)(2,1)S(1)} collective-permute-done((bf16[32,4096]{1,0:T(8,128)(2,1)S(1)}, bf16[32,4096]{1,0:T(8,128)(2,1)S(1)}, u32[]{:S(2)}, u32[]{:S(2)}) %collective-permute-start) | collective-permute-done | bytes 262176 | tf_op jit(solution)/shard_map/while/body/eval_jaxpr/ppermute | solution.py:10
  414.3 8.8 %collective-permute-done = bf16[32,4096]{1,0:T(8,128)(2,1)S(1)} collective-permute-done((bf16[32,4096]{1,0:T(8,128)(2,1)S(1)}, bf16[32,4096]{1,0:T(8,128)(2,1)S(1)}, u32[]{:S(2)}, u32[]{:S(2)}) %collective-permute-start) | collective-permute-done | bytes 262176 | tf_op jit(solution)/shard_map/while/body/eval_jaxpr/ppermute | solution.py:10
  425.6 8.9 %collective-permute-done = bf16[32,4096]{1,0:T(8,128)(2,1)S(1)} collective-permute-done((bf16[32,4096]{1,0:T(8,128)(2,1)S(1)}, bf16[32,4096]{1,0:T(8,128)(2,1)S(1)}, u32[]{:S(2)}, u32[]{:S(2)}) %collective-permute-start) | collective-permute-done | bytes 262176 | tf_op jit(solution)/shard_map/while/body/eval_jaxpr/ppermute | solution.py:10
  437.0 8.8 %collective-permute-done = bf16[32,4096]{1,0:T(8,128)(2,1)S(1)} collective-permute-done((bf16[32,4096]{1,0:T(8,128)(2,1)S(1)}, bf16[32,4096]{1,0:T(8,128)(2,1)S(1)}, u32[]{:S(2)}, u32[]{:S(2)}) %collective-permute-start) | collective-permute-done | bytes 262176 | tf_op jit(solution)/shard_map/while/body/eval_jaxpr/ppermute | solution.py:10
  445.8 1.9 collective-permute-start
  448.3 8.8 %collective-permute-done = bf16[32,4096]{1,0:T(8,128)(2,1)S(1)} collective-permute-done((bf16[32,4096]{1,0:T(8,128)(2,1)S(1)}, bf16[32,4096]{1,0:T(8,128)(2,1)S(1)}, u32[]{:S(2)}, u32[]{:S(2)}) %collective-permute-start) | collective-permute-done | bytes 262176 | tf_op jit(solution)/shard_map/while/body/eval_jaxpr/ppermute | solution.py:10
  457.1 1.9 collective-permute-start
  459.6 8.8 %collective-permute-done = bf16[32,4096]{1,0:T(8,128)(2,1)S(1)} collective-permute-done((bf16[32,4096]{1,0:T(8,128)(2,1)S(1)}, bf16[32,4096]{1,0:T(8,128)(2,1)S(1)}, u32[]{:S(2)}, u32[]{:S(2)}) %collective-permute-start) | collective-permute-done | bytes 262176 | tf_op jit(solution)/shard_map/while/body/eval_jaxpr/ppermute | solution.py:10
  468.5 1.9 collective-permute-start
  470.9 8.9 %collective-permute-done = bf16[32,4096]{1,0:T(8,128)(2,1)S(1)} collective-permute-done((bf16[32,4096]{1,0:T(8,128)(2,1)S(1)}, bf16[32,4096]{1,0:T(8,128)(2,1)S(1)}, u32[]{:S(2)}, u32[]{:S(2)}) %collective-permute-start) | collective-permute-done | bytes 262176 | tf_op jit(solution)/shard_map/while/body/eval_jaxpr/ppermute | solution.py:10
  482.3 8.8 %collective-permute-done = bf16[32,4096]{1,0:T(8,128)(2,1)S(1)} collective-permute-done((bf16[32,4096]{1,0:T(8,128)(2,1)S(1)}, bf16[32,4096]{1,0:T(8,128)(2,1)S(1)}, u32[]{:S(2)}, u32[]{:S(2)}) %collective-permute-start) | collective-permute-done | bytes 262176 | tf_op jit(solution)/shard_map/while/body/eval_jaxpr/ppermute | solution.py:10
  493.6 8.8 %collective-permute-done = bf16[32,4096]{1,0:T(8,128)(2,1)S(1)} collective-permute-done((bf16[32,4096]{1,0:T(8,128)(2,1)S(1)}, bf16[32,4096]{1,0:T(8,128)(2,1)S(1)}, u32[]{:S(2)}, u32[]{:S(2)}) %collective-permute-start) | collective-permute-done | bytes 262176 | tf_op jit(solution)/shard_map/while/body/eval_jaxpr/ppermute | solution.py:10
  504.9 8.8 %collective-permute-done = bf16[32,4096]{1,0:T(8,128)(2,1)S(1)} collective-permute-done((bf16[32,4096]{1,0:T(8,128)(2,1)S(1)}, bf16[32,4096]{1,0:T(8,128)(2,1)S(1)}, u32[]{:S(2)}, u32[]{:S(2)}) %collective-permute-start) | collective-permute-done | bytes 262176 | tf_op jit(solution)/shard_map/while/body/eval_jaxpr/ppermute | solution.py:10
  516.2 8.9 %collective-permute-done = bf16[32,4096]{1,0:T(8,128)(2,1)S(1)} collective-permute-done((bf16[32,4096]{1,0:T(8,128)(2,1)S(1)}, bf16[32,4096]{1,0:T(8,128)(2,1)S(1)}, u32[]{:S(2)}, u32[]{:S(2)}) %collective-permute-start) | collective-permute-done | bytes 262176 | tf_op jit(solution)/shard_map/while/body/eval_jaxpr/ppermute | solution.py:10
  527.6 8.8 %collective-permute-done = bf16[32,4096]{1,0:T(8,128)(2,1)S(1)} collective-permute-done((bf16[32,4096]{1,0:T(8,128)(2,1)S(1)}, bf16[32,4096]{1,0:T(8,128)(2,1)S(1)}, u32[]{:S(2)}, u32[]{:S(2)}) %collective-permute-start) | collective-permute-done | bytes 262176 | tf_op jit(solution)/shard_map/while/body/eval_jaxpr/ppermute | solution.py:10
  538.9 8.8 %collective-permute-done = bf16[32,4096]{1,0:T(8,128)(2,1)S(1)} collective-permute-done((bf16[32,4096]{1,0:T(8,128)(2,1)S(1)}, bf16[32,4096]{1,0:T(8,128)(2,1)S(1)}, u32[]{:S(2)}, u32[]{:S(2)}) %collective-permute-start) | collective-permute-done | bytes 262176 | tf_op jit(solution)/shard_map/while/body/eval_jaxpr/ppermute | solution.py:10
  547.7 1.9 collective-permute-start
  550.2 8.8 %collective-permute-done = bf16[32,4096]{1,0:T(8,128)(2,1)S(1)} collective-permute-done((bf16[32,4096]{1,0:T(8,128)(2,1)S(1)}, bf16[32,4096]{1,0:T(8,128)(2,1)S(1)}, u32[]{:S(2)}, u32[]{:S(2)}) %collective-permute-start) | collective-permute-done | bytes 262176 | tf_op jit(solution)/shard_map/while/body/eval_jaxpr/ppermute | solution.py:10
  559.1 1.9 collective-permute-start
  561.5 8.9 %collective-permute-done = bf16[32,4096]{1,0:T(8,128)(2,1)S(1)} collective-permute-done((bf16[32,4096]{1,0:T(8,128)(2,1)S(1)}, bf16[32,4096]{1,0:T(8,128)(2,1)S(1)}, u32[]{:S(2)}, u32[]{:S(2)}) %collective-permute-start) | collective-permute-done | bytes 262176 | tf_op jit(solution)/shard_map/while/body/eval_jaxpr/ppermute | solution.py:10
  570.4 1.9 collective-permute-start
  572.9 8.8 %collective-permute-done = bf16[32,4096]{1,0:T(8,128)(2,1)S(1)} collective-permute-done((bf16[32,4096]{1,0:T(8,128)(2,1)S(1)}, bf16[32,4096]{1,0:T(8,128)(2,1)S(1)}, u32[]{:S(2)}, u32[]{:S(2)}) %collective-permute-start) | collective-permute-done | bytes 262176 | tf_op jit(solution)/shard_map/while/body/eval_jaxpr/ppermute | solution.py:10
  (141 shorter events, 44.4 us)
Async XLA Ops:
  6.5 52.6 %copy-start = (bf16[128,4096]{1,0:T(8,128)(2,1)S(1)}, bf16[128,4096]{1,0:T(8,128)(2,1)}, u32[]{:S(2)}) copy-start(bf16[128,4096]{1,0:T(8,128)(2,1)} %param.12) | copy-start | bytes 3145732
  6.5 96.2 %all-gather.3.cloned.1.call-start = ((), (), s32[]{:S(2)}) async-start(), calls=%async_computation | async-start | bytes 2162688 | tf_op jit(solution)/shard_map/all_gather | solution.py:47
  112.9 125.4 %copy-start.1 = (bf16[32,4096]{1,0:T(8,128)(2,1)S(1)}, bf16[32,4096]{1,0:T(8,128)(2,1)}, u32[]{:S(2)}) copy-start(bf16[32,4096]{1,0:T(8,128)(2,1)} %param.16) | copy-start | bytes 786436
  238.3 6.1 %collective-permute-start = (bf16[32,4096]{1,0:T(8,128)(2,1)S(1)}, bf16[32,4096]{1,0:T(8,128)(2,1)S(1)}, u32[]{:S(2)}, u32[]{:S(2)}) collective-permute-start(bf16[32,4096]{1,0:T(8,128)(2,1)S(1)} %copy.36), channel_id=1, source_target_pairs={{0,1},{1,2},{2,3},{3,4},{4,5},{5,6},{6,7},{7,8},{8,9},{9,10},{10,1... | collective-permute-start | bytes 786440 | tf_op jit(solution)/shard_map/while/body/eval_jaxpr/ppermute | solution.py:10
  244.4 8.9 %collective-permute-start = (bf16[32,4096]{1,0:T(8,128)(2,1)S(1)}, bf16[32,4096]{1,0:T(8,128)(2,1)S(1)}, u32[]{:S(2)}, u32[]{:S(2)}) collective-permute-start(bf16[32,4096]{1,0:T(8,128)(2,1)S(1)} %copy.36), channel_id=1, source_target_pairs={{0,1},{1,2},{2,3},{3,4},{4,5},{5,6},{6,7},{7,8},{8,9},{9,10},{10,1... | collective-permute-start | bytes 786440 | tf_op jit(solution)/shard_map/while/body/eval_jaxpr/ppermute | solution.py:10
  253.3 11.3 %collective-permute-start = (bf16[32,4096]{1,0:T(8,128)(2,1)S(1)}, bf16[32,4096]{1,0:T(8,128)(2,1)S(1)}, u32[]{:S(2)}, u32[]{:S(2)}) collective-permute-start(bf16[32,4096]{1,0:T(8,128)(2,1)S(1)} %copy.36), channel_id=1, source_target_pairs={{0,1},{1,2},{2,3},{3,4},{4,5},{5,6},{6,7},{7,8},{8,9},{9,10},{10,1... | collective-permute-start | bytes 786440 | tf_op jit(solution)/shard_map/while/body/eval_jaxpr/ppermute | solution.py:10
  264.6 11.3 %collective-permute-start = (bf16[32,4096]{1,0:T(8,128)(2,1)S(1)}, bf16[32,4096]{1,0:T(8,128)(2,1)S(1)}, u32[]{:S(2)}, u32[]{:S(2)}) collective-permute-start(bf16[32,4096]{1,0:T(8,128)(2,1)S(1)} %copy.36), channel_id=1, source_target_pairs={{0,1},{1,2},{2,3},{3,4},{4,5},{5,6},{6,7},{7,8},{8,9},{9,10},{10,1... | collective-permute-start | bytes 786440 | tf_op jit(solution)/shard_map/while/body/eval_jaxpr/ppermute | solution.py:10
  275.9 11.3 %collective-permute-start = (bf16[32,4096]{1,0:T(8,128)(2,1)S(1)}, bf16[32,4096]{1,0:T(8,128)(2,1)S(1)}, u32[]{:S(2)}, u32[]{:S(2)}) collective-permute-start(bf16[32,4096]{1,0:T(8,128)(2,1)S(1)} %copy.36), channel_id=1, source_target_pairs={{0,1},{1,2},{2,3},{3,4},{4,5},{5,6},{6,7},{7,8},{8,9},{9,10},{10,1... | collective-permute-start | bytes 786440 | tf_op jit(solution)/shard_map/while/body/eval_jaxpr/ppermute | solution.py:10
  287.2 11.3 %collective-permute-start = (bf16[32,4096]{1,0:T(8,128)(2,1)S(1)}, bf16[32,4096]{1,0:T(8,128)(2,1)S(1)}, u32[]{:S(2)}, u32[]{:S(2)}) collective-permute-start(bf16[32,4096]{1,0:T(8,128)(2,1)S(1)} %copy.36), channel_id=1, source_target_pairs={{0,1},{1,2},{2,3},{3,4},{4,5},{5,6},{6,7},{7,8},{8,9},{9,10},{10,1... | collective-permute-start | bytes 786440 | tf_op jit(solution)/shard_map/while/body/eval_jaxpr/ppermute | solution.py:10
  298.6 11.3 %collective-permute-start = (bf16[32,4096]{1,0:T(8,128)(2,1)S(1)}, bf16[32,4096]{1,0:T(8,128)(2,1)S(1)}, u32[]{:S(2)}, u32[]{:S(2)}) collective-permute-start(bf16[32,4096]{1,0:T(8,128)(2,1)S(1)} %copy.36), channel_id=1, source_target_pairs={{0,1},{1,2},{2,3},{3,4},{4,5},{5,6},{6,7},{7,8},{8,9},{9,10},{10,1... | collective-permute-start | bytes 786440 | tf_op jit(solution)/shard_map/while/body/eval_jaxpr/ppermute | solution.py:10
  309.9 11.3 %collective-permute-start = (bf16[32,4096]{1,0:T(8,128)(2,1)S(1)}, bf16[32,4096]{1,0:T(8,128)(2,1)S(1)}, u32[]{:S(2)}, u32[]{:S(2)}) collective-permute-start(bf16[32,4096]{1,0:T(8,128)(2,1)S(1)} %copy.36), channel_id=1, source_target_pairs={{0,1},{1,2},{2,3},{3,4},{4,5},{5,6},{6,7},{7,8},{8,9},{9,10},{10,1... | collective-permute-start | bytes 786440 | tf_op jit(solution)/shard_map/while/body/eval_jaxpr/ppermute | solution.py:10
  321.2 11.3 %collective-permute-start = (bf16[32,4096]{1,0:T(8,128)(2,1)S(1)}, bf16[32,4096]{1,0:T(8,128)(2,1)S(1)}, u32[]{:S(2)}, u32[]{:S(2)}) collective-permute-start(bf16[32,4096]{1,0:T(8,128)(2,1)S(1)} %copy.36), channel_id=1, source_target_pairs={{0,1},{1,2},{2,3},{3,4},{4,5},{5,6},{6,7},{7,8},{8,9},{9,10},{10,1... | collective-permute-start | bytes 786440 | tf_op jit(solution)/shard_map/while/body/eval_jaxpr/ppermute | solution.py:10
  332.5 11.3 %collective-permute-start = (bf16[32,4096]{1,0:T(8,128)(2,1)S(1)}, bf16[32,4096]{1,0:T(8,128)(2,1)S(1)}, u32[]{:S(2)}, u32[]{:S(2)}) collective-permute-start(bf16[32,4096]{1,0:T(8,128)(2,1)S(1)} %copy.36), channel_id=1, source_target_pairs={{0,1},{1,2},{2,3},{3,4},{4,5},{5,6},{6,7},{7,8},{8,9},{9,10},{10,1... | collective-permute-start | bytes 786440 | tf_op jit(solution)/shard_map/while/body/eval_jaxpr/ppermute | solution.py:10
  343.9 11.3 %collective-permute-start = (bf16[32,4096]{1,0:T(8,128)(2,1)S(1)}, bf16[32,4096]{1,0:T(8,128)(2,1)S(1)}, u32[]{:S(2)}, u32[]{:S(2)}) collective-permute-start(bf16[32,4096]{1,0:T(8,128)(2,1)S(1)} %copy.36), channel_id=1, source_target_pairs={{0,1},{1,2},{2,3},{3,4},{4,5},{5,6},{6,7},{7,8},{8,9},{9,10},{10,1... | collective-permute-start | bytes 786440 | tf_op jit(solution)/shard_map/while/body/eval_jaxpr/ppermute | solution.py:10
  355.2 11.3 %collective-permute-start = (bf16[32,4096]{1,0:T(8,128)(2,1)S(1)}, bf16[32,4096]{1,0:T(8,128)(2,1)S(1)}, u32[]{:S(2)}, u32[]{:S(2)}) collective-permute-start(bf16[32,4096]{1,0:T(8,128)(2,1)S(1)} %copy.36), channel_id=1, source_target_pairs={{0,1},{1,2},{2,3},{3,4},{4,5},{5,6},{6,7},{7,8},{8,9},{9,10},{10,1... | collective-permute-start | bytes 786440 | tf_op jit(solution)/shard_map/while/body/eval_jaxpr/ppermute | solution.py:10
  366.5 11.3 %collective-permute-start = (bf16[32,4096]{1,0:T(8,128)(2,1)S(1)}, bf16[32,4096]{1,0:T(8,128)(2,1)S(1)}, u32[]{:S(2)}, u32[]{:S(2)}) collective-permute-start(bf16[32,4096]{1,0:T(8,128)(2,1)S(1)} %copy.36), channel_id=1, source_target_pairs={{0,1},{1,2},{2,3},{3,4},{4,5},{5,6},{6,7},{7,8},{8,9},{9,10},{10,1... | collective-permute-start | bytes 786440 | tf_op jit(solution)/shard_map/while/body/eval_jaxpr/ppermute | solution.py:10
  377.8 11.3 %collective-permute-start = (bf16[32,4096]{1,0:T(8,128)(2,1)S(1)}, bf16[32,4096]{1,0:T(8,128)(2,1)S(1)}, u32[]{:S(2)}, u32[]{:S(2)}) collective-permute-start(bf16[32,4096]{1,0:T(8,128)(2,1)S(1)} %copy.36), channel_id=1, source_target_pairs={{0,1},{1,2},{2,3},{3,4},{4,5},{5,6},{6,7},{7,8},{8,9},{9,10},{10,1... | collective-permute-start | bytes 786440 | tf_op jit(solution)/shard_map/while/body/eval_jaxpr/ppermute | solution.py:10
  389.2 11.3 %collective-permute-start = (bf16[32,4096]{1,0:T(8,128)(2,1)S(1)}, bf16[32,4096]{1,0:T(8,128)(2,1)S(1)}, u32[]{:S(2)}, u32[]{:S(2)}) collective-permute-start(bf16[32,4096]{1,0:T(8,128)(2,1)S(1)} %copy.36), channel_id=1, source_target_pairs={{0,1},{1,2},{2,3},{3,4},{4,5},{5,6},{6,7},{7,8},{8,9},{9,10},{10,1... | collective-permute-start | bytes 786440 | tf_op jit(solution)/shard_map/while/body/eval_jaxpr/ppermute | solution.py:10
  400.5 11.3 %collective-permute-start = (bf16[32,4096]{1,0:T(8,128)(2,1)S(1)}, bf16[32,4096]{1,0:T(8,128)(2,1)S(1)}, u32[]{:S(2)}, u32[]{:S(2)}) collective-permute-start(bf16[32,4096]{1,0:T(8,128)(2,1)S(1)} %copy.36), channel_id=1, source_target_pairs={{0,1},{1,2},{2,3},{3,4},{4,5},{5,6},{6,7},{7,8},{8,9},{9,10},{10,1... | collective-permute-start | bytes 786440 | tf_op jit(solution)/shard_map/while/body/eval_jaxpr/ppermute | solution.py:10
  411.8 11.3 %collective-permute-start = (bf16[32,4096]{1,0:T(8,128)(2,1)S(1)}, bf16[32,4096]{1,0:T(8,128)(2,1)S(1)}, u32[]{:S(2)}, u32[]{:S(2)}) collective-permute-start(bf16[32,4096]{1,0:T(8,128)(2,1)S(1)} %copy.36), channel_id=1, source_target_pairs={{0,1},{1,2},{2,3},{3,4},{4,5},{5,6},{6,7},{7,8},{8,9},{9,10},{10,1... | collective-permute-start | bytes 786440 | tf_op jit(solution)/shard_map/while/body/eval_jaxpr/ppermute | solution.py:10
  423.2 11.3 %collective-permute-start = (bf16[32,4096]{1,0:T(8,128)(2,1)S(1)}, bf16[32,4096]{1,0:T(8,128)(2,1)S(1)}, u32[]{:S(2)}, u32[]{:S(2)}) collective-permute-start(bf16[32,4096]{1,0:T(8,128)(2,1)S(1)} %copy.36), channel_id=1, source_target_pairs={{0,1},{1,2},{2,3},{3,4},{4,5},{5,6},{6,7},{7,8},{8,9},{9,10},{10,1... | collective-permute-start | bytes 786440 | tf_op jit(solution)/shard_map/while/body/eval_jaxpr/ppermute | solution.py:10
  434.5 11.3 %collective-permute-start = (bf16[32,4096]{1,0:T(8,128)(2,1)S(1)}, bf16[32,4096]{1,0:T(8,128)(2,1)S(1)}, u32[]{:S(2)}, u32[]{:S(2)}) collective-permute-start(bf16[32,4096]{1,0:T(8,128)(2,1)S(1)} %copy.36), channel_id=1, source_target_pairs={{0,1},{1,2},{2,3},{3,4},{4,5},{5,6},{6,7},{7,8},{8,9},{9,10},{10,1... | collective-permute-start | bytes 786440 | tf_op jit(solution)/shard_map/while/body/eval_jaxpr/ppermute | solution.py:10
  445.8 11.3 %collective-permute-start = (bf16[32,4096]{1,0:T(8,128)(2,1)S(1)}, bf16[32,4096]{1,0:T(8,128)(2,1)S(1)}, u32[]{:S(2)}, u32[]{:S(2)}) collective-permute-start(bf16[32,4096]{1,0:T(8,128)(2,1)S(1)} %copy.36), channel_id=1, source_target_pairs={{0,1},{1,2},{2,3},{3,4},{4,5},{5,6},{6,7},{7,8},{8,9},{9,10},{10,1... | collective-permute-start | bytes 786440 | tf_op jit(solution)/shard_map/while/body/eval_jaxpr/ppermute | solution.py:10
  457.1 11.3 %collective-permute-start = (bf16[32,4096]{1,0:T(8,128)(2,1)S(1)}, bf16[32,4096]{1,0:T(8,128)(2,1)S(1)}, u32[]{:S(2)}, u32[]{:S(2)}) collective-permute-start(bf16[32,4096]{1,0:T(8,128)(2,1)S(1)} %copy.36), channel_id=1, source_target_pairs={{0,1},{1,2},{2,3},{3,4},{4,5},{5,6},{6,7},{7,8},{8,9},{9,10},{10,1... | collective-permute-start | bytes 786440 | tf_op jit(solution)/shard_map/while/body/eval_jaxpr/ppermute | solution.py:10
  468.5 11.3 %collective-permute-start = (bf16[32,4096]{1,0:T(8,128)(2,1)S(1)}, bf16[32,4096]{1,0:T(8,128)(2,1)S(1)}, u32[]{:S(2)}, u32[]{:S(2)}) collective-permute-start(bf16[32,4096]{1,0:T(8,128)(2,1)S(1)} %copy.36), channel_id=1, source_target_pairs={{0,1},{1,2},{2,3},{3,4},{4,5},{5,6},{6,7},{7,8},{8,9},{9,10},{10,1... | collective-permute-start | bytes 786440 | tf_op jit(solution)/shard_map/while/body/eval_jaxpr/ppermute | solution.py:10
  479.8 11.3 %collective-permute-start = (bf16[32,4096]{1,0:T(8,128)(2,1)S(1)}, bf16[32,4096]{1,0:T(8,128)(2,1)S(1)}, u32[]{:S(2)}, u32[]{:S(2)}) collective-permute-start(bf16[32,4096]{1,0:T(8,128)(2,1)S(1)} %copy.36), channel_id=1, source_target_pairs={{0,1},{1,2},{2,3},{3,4},{4,5},{5,6},{6,7},{7,8},{8,9},{9,10},{10,1... | collective-permute-start | bytes 786440 | tf_op jit(solution)/shard_map/while/body/eval_jaxpr/ppermute | solution.py:10
  491.1 11.3 %collective-permute-start = (bf16[32,4096]{1,0:T(8,128)(2,1)S(1)}, bf16[32,4096]{1,0:T(8,128)(2,1)S(1)}, u32[]{:S(2)}, u32[]{:S(2)}) collective-permute-start(bf16[32,4096]{1,0:T(8,128)(2,1)S(1)} %copy.36), channel_id=1, source_target_pairs={{0,1},{1,2},{2,3},{3,4},{4,5},{5,6},{6,7},{7,8},{8,9},{9,10},{10,1... | collective-permute-start | bytes 786440 | tf_op jit(solution)/shard_map/while/body/eval_jaxpr/ppermute | solution.py:10
  502.4 11.3 %collective-permute-start = (bf16[32,4096]{1,0:T(8,128)(2,1)S(1)}, bf16[32,4096]{1,0:T(8,128)(2,1)S(1)}, u32[]{:S(2)}, u32[]{:S(2)}) collective-permute-start(bf16[32,4096]{1,0:T(8,128)(2,1)S(1)} %copy.36), channel_id=1, source_target_pairs={{0,1},{1,2},{2,3},{3,4},{4,5},{5,6},{6,7},{7,8},{8,9},{9,10},{10,1... | collective-permute-start | bytes 786440 | tf_op jit(solution)/shard_map/while/body/eval_jaxpr/ppermute | solution.py:10
  513.8 11.3 %collective-permute-start = (bf16[32,4096]{1,0:T(8,128)(2,1)S(1)}, bf16[32,4096]{1,0:T(8,128)(2,1)S(1)}, u32[]{:S(2)}, u32[]{:S(2)}) collective-permute-start(bf16[32,4096]{1,0:T(8,128)(2,1)S(1)} %copy.36), channel_id=1, source_target_pairs={{0,1},{1,2},{2,3},{3,4},{4,5},{5,6},{6,7},{7,8},{8,9},{9,10},{10,1... | collective-permute-start | bytes 786440 | tf_op jit(solution)/shard_map/while/body/eval_jaxpr/ppermute | solution.py:10
  525.1 11.3 %collective-permute-start = (bf16[32,4096]{1,0:T(8,128)(2,1)S(1)}, bf16[32,4096]{1,0:T(8,128)(2,1)S(1)}, u32[]{:S(2)}, u32[]{:S(2)}) collective-permute-start(bf16[32,4096]{1,0:T(8,128)(2,1)S(1)} %copy.36), channel_id=1, source_target_pairs={{0,1},{1,2},{2,3},{3,4},{4,5},{5,6},{6,7},{7,8},{8,9},{9,10},{10,1... | collective-permute-start | bytes 786440 | tf_op jit(solution)/shard_map/while/body/eval_jaxpr/ppermute | solution.py:10
  536.4 11.3 %collective-permute-start = (bf16[32,4096]{1,0:T(8,128)(2,1)S(1)}, bf16[32,4096]{1,0:T(8,128)(2,1)S(1)}, u32[]{:S(2)}, u32[]{:S(2)}) collective-permute-start(bf16[32,4096]{1,0:T(8,128)(2,1)S(1)} %copy.36), channel_id=1, source_target_pairs={{0,1},{1,2},{2,3},{3,4},{4,5},{5,6},{6,7},{7,8},{8,9},{9,10},{10,1... | collective-permute-start | bytes 786440 | tf_op jit(solution)/shard_map/while/body/eval_jaxpr/ppermute | solution.py:10
  547.7 11.3 %collective-permute-start = (bf16[32,4096]{1,0:T(8,128)(2,1)S(1)}, bf16[32,4096]{1,0:T(8,128)(2,1)S(1)}, u32[]{:S(2)}, u32[]{:S(2)}) collective-permute-start(bf16[32,4096]{1,0:T(8,128)(2,1)S(1)} %copy.36), channel_id=1, source_target_pairs={{0,1},{1,2},{2,3},{3,4},{4,5},{5,6},{6,7},{7,8},{8,9},{9,10},{10,1... | collective-permute-start | bytes 786440 | tf_op jit(solution)/shard_map/while/body/eval_jaxpr/ppermute | solution.py:10
  559.1 11.3 %collective-permute-start = (bf16[32,4096]{1,0:T(8,128)(2,1)S(1)}, bf16[32,4096]{1,0:T(8,128)(2,1)S(1)}, u32[]{:S(2)}, u32[]{:S(2)}) collective-permute-start(bf16[32,4096]{1,0:T(8,128)(2,1)S(1)} %copy.36), channel_id=1, source_target_pairs={{0,1},{1,2},{2,3},{3,4},{4,5},{5,6},{6,7},{7,8},{8,9},{9,10},{10,1... | collective-permute-start | bytes 786440 | tf_op jit(solution)/shard_map/while/body/eval_jaxpr/ppermute | solution.py:10
  570.4 11.3 %collective-permute-start = (bf16[32,4096]{1,0:T(8,128)(2,1)S(1)}, bf16[32,4096]{1,0:T(8,128)(2,1)S(1)}, u32[]{:S(2)}, u32[]{:S(2)}) collective-permute-start(bf16[32,4096]{1,0:T(8,128)(2,1)S(1)} %copy.36), channel_id=1, source_target_pairs={{0,1},{1,2},{2,3},{3,4},{4,5},{5,6},{6,7},{7,8},{8,9},{9,10},{10,1... | collective-permute-start | bytes 786440 | tf_op jit(solution)/shard_map/while/body/eval_jaxpr/ppermute | solution.py:10
  581.7 0.6 copy-start.2
Sparse Core Ops, SparseCore 0:
  10.7 91.9 all-gather.2
where the time goes:
time: 600 us; the launch traced here: 591 us
  waiting for transfers between devices  306 us (51%)
  blocking collectives  147 us (24%)
  starting transfers between devices  64.1 us (11%)
  other arithmetic  25.8 us (4%)
  matrix products  17.1 us (3%)
  local copies, waits for them, and re-layouts  15 us (2%)
  between operations  14.8 us (2%)
    ppermute x31, waiting for transfers between devices, passed_along(): return lax.ppermute(value, axis, pairs)  262 us
    psum x1, blocking collectives, on_device(): lax.psum(jnp.stack([in_partial, out_partial]), ('dp', 'query')) / tokens_all  95.8 us
    ppermute x31, starting transfers between devices, passed_along(): return lax.ppermute(value, axis, pairs)  64.1 us
    all_gather x1, blocking collectives, on_device(): lax.all_gather(out_projection, 'query', axis=1, tiled=True)  51.1 us
    all_gather x1, waiting for transfers between devices, on_device(): lax.all_gather(in_projection, 'query', axis=1, tiled=True)  42.8 us
    another operation x6, other arithmetic, damped_inverse(): lower_factor = jnp.linalg.cholesky(damped)  13.2 us
  transfers between devices with their start and end apart: 32, of which 32 were waited for; matrix products, arithmetic and copies ran while one was open for 3% of the time, Pallas kernels for 0%

commit v1 on v0

v1 whole, which is shorter than its diff:
```python
import functools

import jax
import jax.numpy as jnp
from jax import lax
from jax.experimental import pallas as pl
from jax.experimental.pallas import tpu as pltpu
from jax.sharding import PartitionSpec as P

MESH = pl.DeviceIdType.MESH
RANK = 64
SEQ = 16
TOK = 128
IN_COLS = 448
IN_PAD = 512
OUT_COLS = 128
BLK = IN_PAD + OUT_COLS
Q_ROWS = 32
NT = (((1,), (1,)), ((), ()))
NN = (((1,), (0,)), ((), ()))
HIGHEST = lax.Precision.HIGHEST


def dot(a, b, dims=NN, precision=None):
    return lax.dot_general(a, b, dims, precision=precision, preferred_element_type=jnp.float32)


def split(x):
    hi = x.astype(jnp.bfloat16)
    return hi, (x - hi.astype(jnp.float32)).astype(jnp.bfloat16)


def damped_inverses(total, tokens):
    lane = lax.broadcasted_iota(jnp.int32, (RANK, TOK), 1)
    row = lax.broadcasted_iota(jnp.int32, (RANK, TOK), 0)
    mean = total * (1.0 / tokens)
    done = []
    for work in (mean, pltpu.roll(mean, RANK, 1)):
        diagonal = row == lane
        trace = jnp.sum(jnp.where(diagonal, work, 0.0))
        work = jnp.where(lane < RANK, work, 0.0)
        done.append(jnp.where(diagonal, work + 0.1 * trace / RANK, work))
    one, two = done
    lane1 = lax.broadcasted_iota(jnp.int32, (1, TOK), 1)
    for k in range(RANK):
        new = []
        for work in (one, two):
            pivot_row = work[k : k + 1, :]
            inverse = 1.0 / pivot_row[:, k : k + 1]
            scaled = jnp.where(lane1 == k, inverse, pivot_row * inverse)
            update = jnp.where(lane == k, 0.0, work) - work[:, k : k + 1] * scaled
            new.append(jnp.where(row == k, scaled, update))
        one, two = new
    return one, two


def kernel(
    Y, Z, tokens,
    acts_hbm, outg_hbm, inp_ref, outp_ref, len_ref, q_hbm,
    out_ref,
    acts, outg, qraw, stage, gath, qall, tok, part, total, ar1, ar2, ar3, mine, gsc, sco, ret,
    loc_sem, z_send, z_recv, cx_send, cx_recv, pt_send, pt_recv, sb_send, sb_recv,
    t_send, t_recv, q_send, q_recv, a_send, a_recv,
):
    H = Z // 2
    dpi, qi = lax.axis_index("dp"), lax.axis_index("query")
    y, xl = dpi // 2, dpi % 2
    xh, z, c = qi // (2 * Z), (qi // 2) % Z, qi % 2

    def at(y_, xl_, xh_, z_, c_):
        return (y_ * 2 + xl_, xh_ * (2 * Z) + z_ * 2 + c_)

    def zp(off):
        return (z + (off + Z)) % Z

    def z_peer(off):
        return at(y, xl, xh, zp(off), c)

    def y_peer(off):
        return at((y + off) % Y, xl, xh, z, c)

    def x_peer(m):
        return at(y, (xl + (m // 2) % 2) % 2, (xh + m // 4) % 2, z, (c + m % 2) % 2)

    cross = at(y, 1 - xl, 1 - xh, z, c)
    partner = at(y, 1 - xl, xh, z, c)
    sibling = at(y, xl, xh, z, 1 - c)

    pending = []

    def push(ref_src, ref_dst, send, recv, to):
        copy = pltpu.make_async_remote_copy(
            src_ref=ref_src, dst_ref=ref_dst, send_sem=send, recv_sem=recv, device_id=to, device_id_type=MESH
        )
        copy.start()
        pending.append(copy)

    def got(ref, sem):
        pltpu.make_async_copy(ref, ref, sem).wait()

    loads = [
        pltpu.make_async_copy(acts_hbm, acts, loc_sem.at[0]),
        pltpu.make_async_copy(outg_hbm, outg, loc_sem.at[1]),
        pltpu.make_async_copy(q_hbm, qraw, loc_sem.at[2]),
    ]
    for load in loads:
        load.start()
    barrier = pltpu.get_barrier_semaphore()
    peers = [z_peer(d) for d in range(1, Z)] + [x_peer(m) for m in range(1, 8)] + [y_peer(d) for d in range(1, Y)]
    for peer in peers:
        pl.semaphore_signal(barrier, inc=1, device_id=peer, device_id_type=MESH)

    def block_of(h, zz, cc):
        return h * (2 * Z) + zz * 2 + cc

    def whole(b):
        return gath.at[pl.ds(pl.multiple_of(b * RANK, RANK), RANK), :]

    def piece(b, p):
        return gath.at[pl.ds(pl.multiple_of(b * RANK + p * 32, 32), 32), :]

    own = block_of(xh, z, c)
    stage[...] = jnp.zeros_like(stage)
    stage[:, 0:IN_COLS] = inp_ref[...].astype(jnp.float32)
    plain = stage[...]
    shifted = pltpu.roll(plain, IN_PAD - IN_COLS, 1)
    own_rows = pl.ds(pl.multiple_of(own * RANK, RANK), RANK)
    gath[own_rows, 0:IN_PAD] = jnp.where(c == 1, shifted, plain).astype(jnp.bfloat16)
    gath[own_rows, IN_PAD:BLK] = outp_ref[...]
    pl.semaphore_wait(barrier, len(peers))

    offs = [0]
    for s in range(1, H):
        offs += [-s, s]
    offs.append(H)

    def z_forward(k, ref_of, send, recv):
        off = offs[k]
        dist = abs(off)
        for way, sign in ((0, 1), (1, -1)):
            goes = (k == 0) or (k != Z - 1 and (off < 0) == (sign > 0))
            if not goes:
                continue
            for p in (0, 1):
                if dist + 1 == H and p != way:
                    continue
                ref = ref_of(zp(off), p)
                push(ref, ref, send.at[way, dist, p], recv.at[way, dist, p], z_peer(sign))

    def z_wait(k, ref_of, recv):
        off = offs[k]
        dist = abs(off)
        if dist == 0:
            return
        for p in (0, 1):
            if dist == H:
                way = p
            else:
                way = 0 if off < 0 else 1
            got(ref_of(zp(off), p), recv.at[way, dist - 1, p])

    def gath_piece(zz, p):
        return piece(block_of(xh, zz, c), p)

    sums = [jnp.zeros((RANK, TOK), jnp.float32), jnp.zeros((RANK, TOK), jnp.float32)]

    def fold(h, zz, cc):
        b = block_of(h, zz, cc)
        rows = pl.ds(pl.multiple_of(b * RANK, RANK), RANK)
        first = pl.multiple_of((h * Z + zz) * (2 * IN_COLS) + cc * 384, 128)
        sums[0] = sums[0] + dot(gath[rows, 0:IN_PAD], acts[:, pl.ds(first, IN_PAD)], NT)
        second = pl.multiple_of(b * OUT_COLS, OUT_COLS)
        sums[1] = sums[1] + dot(gath[rows, IN_PAD:BLK], outg[:, pl.ds(second, OUT_COLS)], NT)

    for tick in range(Z + 4):
        if tick < Z:
            zz = zp(offs[tick])
            z_wait(tick, gath_piece, z_recv)
            z_forward(tick, gath_piece, z_send, z_recv)
            ref = piece(block_of(xh, zz, c), xl)
            push(ref, ref, cx_send.at[tick], cx_recv.at[tick], cross)
            ref = whole(block_of(xh, zz, c))
            push(ref, ref, sb_send.at[tick, 0], sb_recv.at[tick, 0], sibling)
        k = tick - 1
        if 0 <= k < Z:
            ref = piece(block_of(1 - xh, zp(offs[k]), c), 1 - xl)
            got(ref, cx_recv.at[k])
            push(ref, ref, pt_send.at[k], pt_recv.at[k], partner)
            push(ref, ref, sb_send.at[k, 1], sb_recv.at[k, 1], sibling)
        k = tick - 2
        if 0 <= k < Z:
            ref = piece(block_of(1 - xh, zp(offs[k]), c), xl)
            got(ref, pt_recv.at[k])
            push(ref, ref, sb_send.at[k, 2], sb_recv.at[k, 2], sibling)
        if tick == 0:
            loads[0].wait()
            loads[1].wait()
        if tick < Z:
            fold(xh, zp(offs[tick]), c)
        k = tick - 2
        if 0 <= k < Z:
            zz = zp(offs[k])
            fold(1 - xh, zz, c)
            got(whole(block_of(xh, zz, 1 - c)), sb_recv.at[k, 0])
            fold(xh, zz, 1 - c)
        k = tick - 4
        if 0 <= k < Z:
            zz = zp(offs[k])
            got(piece(block_of(1 - xh, zz, 1 - c), 1 - xl), sb_recv.at[k, 1])
            got(piece(block_of(1 - xh, zz, 1 - c), xl), sb_recv.at[k, 2])
            fold(1 - xh, zz, 1 - c)

    lane1 = lax.broadcasted_iota(jnp.int32, (1, TOK), 1)
    counts = jnp.zeros((1, TOK), jnp.int32)
    for e in range(TOK // SEQ):
        counts = jnp.where(lane1 // SEQ == e, len_ref[e], counts)
    live = (lane1 % SEQ < counts).astype(jnp.float32)
    masked = jnp.concatenate(sums, axis=0) * live
    own_tok = pl.ds(pl.multiple_of(z * TOK, TOK), TOK)
    tok[own_tok, :] = masked
    gram = dot(masked, masked, NT, HIGHEST)
    lane = lax.broadcasted_iota(jnp.int32, (RANK, TOK), 1)
    part[...] = jnp.where(lane < RANK, gram[0:RANK], gram[RANK:])

    rows_z = RANK // Z

    def z_rows(zz):
        return pl.ds(pl.multiple_of(zz * rows_z, rows_z), rows_z)

    def tok_piece(zz, p):
        return tok.at[pl.ds(pl.multiple_of(zz * TOK + p * RANK, RANK), RANK), :]

    def tok_step(k):
        z_wait(k, tok_piece, t_recv)
        z_forward(k, tok_piece, t_send, t_recv)

    for d in range(1, Z):
        push(part.at[z_rows(zp(d)), :], ar1.at[d - 1], a_send.at[0, d - 1], a_recv.at[0], z_peer(d))
    tok_step(0)
    lane_q = lax.broadcasted_iota(jnp.int32, (Q_ROWS, TOK), 1)
    loads[2].wait()
    q_cols = qraw.shape[1]

    def q_slot(h, cc):
        return (h * 2 + cc) * Q_ROWS

    def q_piece(h, cc, p):
        half = Q_ROWS // 2
        return qall.at[pl.ds(pl.multiple_of(q_slot(h, cc) + p * half, half), half), :]

    own_q = pl.ds(pl.multiple_of(q_slot(xh, c), Q_ROWS), Q_ROWS)
    for m in range(q_cols // 256):
        first = qraw[:, 128 * m : 128 * m + 128].astype(jnp.float32)
        second = qraw[:, q_cols // 2 + 128 * m : q_cols // 2 + 128 * m + 128].astype(jnp.float32)
        low = jnp.where(lane_q < RANK, first, pltpu.roll(second, RANK, 1))
        high = jnp.where(lane_q < RANK, pltpu.roll(first, RANK, 1), second)
        qall[own_q, 256 * m : 256 * m + 128] = low.astype(jnp.bfloat16)
        qall[own_q, 256 * m + 128 : 256 * m + 256] = high.astype(jnp.bfloat16)
    ref = q_piece(xh, c, xl)
    push(ref, ref, q_send.at[0], q_recv.at[0], cross)
    ref = qall.at[own_q, :]
    push(ref, ref, q_send.at[1], q_recv.at[1], sibling)

    got(ar1, a_recv.at[0])
    summed = part[z_rows(z), :]
    for d in range(Z - 1):
        summed = summed + ar1[d]
    mine[0] = summed
    for m in range(1, 8):
        push(mine.at[0], ar2.at[m - 1], a_send.at[1, m - 1], a_recv.at[1], x_peer(m))
    for k in range(1, min(3, Z)):
        tok_step(k)
    got(ar2, a_recv.at[1])
    for m in range(7):
        summed = summed + ar2[m]
    mine[1] = summed
    for d in range(1, Y):
        push(mine.at[1], ar3.at[d - 1], a_send.at[2, d - 1], a_recv.at[2], y_peer(d))
    for k in range(3, min(5, Z)):
        tok_step(k)
    got(ar3, a_recv.at[2])
    for d in range(Y - 1):
        summed = summed + ar3[d]
    total[z_rows(z), :] = summed
    for d in range(1, Z):
        here = total.at[z_rows(z), :]
        push(here, here, a_send.at[3, d - 1], a_recv.at[3], z_peer(d))
    for k in range(5, Z):
        tok_step(k)
    ref = q_piece(1 - xh, c, 1 - xl)
    got(ref, q_recv.at[0])
    push(ref, ref, q_send.at[2], q_recv.at[2], partner)
    push(ref, ref, q_send.at[3], q_recv.at[3], sibling)
    got(total.at[0 : RANK - rows_z, :], a_recv.at[3])

    in_inverse, out_inverse = damped_inverses(total[...], tokens)

    ref = q_piece(1 - xh, c, xl)
    got(ref, q_recv.at[2])
    push(ref, ref, q_send.at[4], q_recv.at[4], sibling)

    example = lax.broadcasted_iota(jnp.int32, (SEQ // 2, TOK), 0)
    token = lax.broadcasted_iota(jnp.int32, (SEQ // 2, TOK), 1)
    belongs = (token // SEQ == example).astype(jnp.float32)
    nothing = jnp.zeros((RANK, TOK), jnp.bfloat16)
    half = RANK // 2
    for k in range(Z):
        ins = dot(in_inverse[:, 0:RANK], tok[k * TOK : k * TOK + RANK, :], NN, HIGHEST)
        outs = dot(out_inverse[:, 0:RANK], tok[k * TOK + RANK : (k + 1) * TOK, :], NN, HIGHEST)
        left, right = [], []
        for w in split(outs):
            spread = (w.astype(jnp.float32)[:, None, :] * belongs[None, :, :]).astype(jnp.bfloat16)
            spread = spread.reshape(RANK * 8, TOK)
            left.append(jnp.concatenate([spread[0 : half * 8], spread[half * 8 :]], axis=1))
        for w in split(ins):
            right.append(
                jnp.concatenate(
                    [jnp.concatenate([w, nothing], axis=1), jnp.concatenate([nothing, w], axis=1)], axis=0
                )
            )
        grads = dot(left[0], right[0], NT) + (dot(left[0], right[1], NT) + dot(left[1], right[0], NT))
        gsc[:, k * 8 : (k + 1) * 8, :] = grads.reshape(half, 8, TOK)

    got(qall.at[pl.ds(pl.multiple_of(q_slot(xh, 1 - c), Q_ROWS), Q_ROWS), :], q_recv.at[1])
    got(q_piece(1 - xh, 1 - c, 1 - xl), q_recv.at[3])
    got(q_piece(1 - xh, 1 - c, xl), q_recv.at[4])
    scores = jnp.zeros((2 * 8 * Z, TOK), jnp.float32)
    for m in range(half // 2):
        both = jnp.concatenate([gsc[2 * m], gsc[2 * m + 1]], axis=1)
        hi, lo = split(both)
        scores = scores + dot(jnp.concatenate([hi, lo], axis=0), qall[:, 256 * m : 256 * m + 256], NT)
    sco[...] = scores[0 : 8 * Z] + scores[8 * Z :]
    for d in range(1, Z):
        push(
            sco.at[pl.ds(pl.multiple_of(zp(d) * 8, 8), 8), :], ret.at[d], a_send.at[4, d - 1], a_recv.at[4], z_peer(d)
        )
    ret[0] = sco[pl.ds(pl.multiple_of(z * 8, 8), 8), :]
    got(ret.at[1:Z], a_recv.at[4])
    lane8 = lax.broadcasted_iota(jnp.int32, (8, TOK), 1)
    width = Z * RANK
    for m in range(Z // 2):
        first = ret[zp(-2 * m)]
        second = ret[zp(-2 * m - 1)]
        out_ref[:, 128 * m : 128 * m + 128] = jnp.where(lane8 < RANK, first, pltpu.roll(second, RANK, 1))
        out_ref[:, width + 128 * m : width + 128 * m + 128] = jnp.where(
            lane8 < RANK, pltpu.roll(first, RANK, 1), second
        )
    for copy in pending:
        copy.wait_send()


def solution(mesh):
    Y, Z = mesh.shape["dp"] // 2, mesh.shape["query"] // 4
    H = Z // 2

    def on_device(activations, out_grads, in_projection, out_projection, lengths, queries):
        tokens = activations.shape[0] * mesh.shape["dp"] * mesh.shape["query"]
        f32, bf16 = jnp.float32, jnp.bfloat16
        vmem = pl.BlockSpec(memory_space=pltpu.VMEM)
        hbm = pl.BlockSpec(memory_space=pl.ANY)
        sem = pltpu.SemaphoreType.DMA
        return pl.pallas_call(
            functools.partial(kernel, Y, Z, tokens),
            out_shape=jax.ShapeDtypeStruct((lengths.shape[0], Z * 4 * Q_ROWS), f32),
            in_specs=[hbm, hbm, vmem, vmem, pl.BlockSpec(memory_space=pltpu.SMEM), hbm],
            out_specs=vmem,
            scratch_shapes=[
                pltpu.VMEM(activations.shape, bf16),
                pltpu.VMEM(out_grads.shape, bf16),
                pltpu.VMEM(queries.shape, bf16),
                pltpu.VMEM((RANK, IN_PAD), f32),
                pltpu.VMEM((4 * Z * RANK, BLK), bf16),
                pltpu.VMEM((4 * Q_ROWS, queries.shape[1]), bf16),
                pltpu.VMEM((Z * TOK, TOK), f32),
                pltpu.VMEM((RANK, TOK), f32),
                pltpu.VMEM((RANK, TOK), f32),
                pltpu.VMEM((Z - 1, RANK // Z, TOK), f32),
                pltpu.VMEM((7, RANK // Z, TOK), f32),
                pltpu.VMEM((Y - 1, RANK // Z, TOK), f32),
                pltpu.VMEM((2, RANK // Z, TOK), f32),
                pltpu.VMEM((RANK // 2, 8 * Z, TOK), f32),
                pltpu.VMEM((8 * Z, TOK), f32),
                pltpu.VMEM((Z, 8, TOK), f32),
                sem((3,)),
                sem((2, H, 2)),
                sem((2, H, 2)),
                sem((Z,)),
                sem((Z,)),
                sem((Z,)),
                sem((Z,)),
                sem((Z, 3)),
                sem((Z, 3)),
                sem((2, H, 2)),
                sem((2, H, 2)),
                sem((5,)),
                sem((5,)),
                sem((5, 7)),
                sem((5,)),
            ],
            compiler_params=pltpu.CompilerParams(
                collective_id=0, has_side_effects=True, vmem_limit_bytes=50 * 1024 * 1024
            ),
        )(activations, out_grads, in_projection, out_projection, lengths, queries)

    placed = (
        P(("dp", "query"), None),
        P(("dp", "query"), None),
        P(None, "query"),
        P(None, "query"),
        P(("dp", "query")),
        P("query", None),
    )
    return jax.shard_map(
        on_device, mesh=mesh, in_specs=placed, out_specs=P(("dp", "query"), None), check_vma=False
    )
```

time: 600 us -> 79.5 us (0.13); the launches traced: 591 us -> 78.3 us
  waiting for transfers between devices: 306 us -> 0 us
  blocking collectives: 147 us -> 0 us
  Pallas kernels: 0 us -> 73.3 us
  starting transfers between devices: 64.1 us -> 0 us
  other arithmetic: 25.8 us -> 0 us
  matrix products: 17.1 us -> 0 us
  between operations: 14.8 us -> 0.01 us
  local copies, waits for them, and re-layouts: 15 us -> 5 us
    ppermute x31 -> x0, waiting for transfers between devices: 262 us -> none  [passed_along(): return lax.ppermute(value, axis, pairs)]
    psum x1 -> x0, blocking collectives: 95.8 us -> none  [on_device(): lax.psum(jnp.stack([in_partial, out_partial]), ('dp', 'query')) / tokens_all]
    pallas_call x0 -> x1, Pallas kernels: none -> 73.3 us  [on_device(): pl.pallas_call(functools.partial(kernel, Y, Z, tokens), out_shape=jax.Sha...]
    ppermute x31 -> x0, starting transfers between devices: 64.1 us -> none  [passed_along(): return lax.ppermute(value, axis, pairs)]
    all_gather x1 -> x0, blocking collectives: 51.1 us -> none  [on_device(): lax.all_gather(out_projection, 'query', axis=1, tiled=True)]
    all_gather x1 -> x0, waiting for transfers between devices: 42.8 us -> none  [on_device(): lax.all_gather(in_projection, 'query', axis=1, tiled=True)]
    another operation x11 -> x0, other arithmetic: 24.4 us -> none  [the longest x6 13.2 us: damped_inverse(): lower_factor = jnp.linalg.cholesky(damped)]
    dot_general x41 -> x0, matrix products: 16.6 us -> none  [the longest x32 9.75 us: score_block(): lax.dot_general(preconditioned, query_block.astype(jnp.float32), (((1,),...]
  transfers between devices with their start and end apart: 32 -> 0, of which waited for: 32 -> 0; matrix products, arithmetic and copies ran while one was open for 3% -> 0% of each run, Pallas kernels for 0% -> 0%
where the time goes in v1:
time: 79.5 us; the launch traced here: 78.3 us
  Pallas kernels  73.3 us (92%)
  local copies, waits for them, and re-layouts  5 us (6%)
    pallas_call x1, Pallas kernels, on_device(): pl.pallas_call(functools.partial(kernel, Y, Z, tokens), out_shape=jax.Sha...  73.3 us
    unnamed x11, local copies, waits for them, and re-layouts  5 us

profile of v1, /device:TPU:1, one launch (start us, length us, event | category | flops | bytes accessed | tf_op | source)
XLA Modules:
  0.0 78.3 jit_solution(1836193385841431782)
XLA Ops:
  0.0 0.0 copy-start
  0.0 1.2 %copy-done = bf16[128,4096]{1,0:T(8,128)(2,1)S(1)} copy-done((bf16[128,4096]{1,0:T(8,128)(2,1)S(1)}, bf16[128,4096]{1,0:T(8,128)(2,1)}, u32[]{:S(2)}) %copy-start) | copy-done | bytes 1048600
  1.2 0.0 copy-start.1
  1.2 0.9 %copy-done.1 = bf16[32,4096]{1,0:T(8,128)(2,1)S(1)} copy-done((bf16[32,4096]{1,0:T(8,128)(2,1)S(1)}, bf16[32,4096]{1,0:T(8,128)(2,1)}, u32[]{:S(2)}) %copy-start.1) | copy-done | bytes 262168
  2.2 0.0 copy-start.2
  2.2 0.8 %copy-done.2 = bf16[64,448]{1,0:T(8,128)(2,1)S(1)} copy-done((bf16[64,448]{1,0:T(8,128)(2,1)S(1)}, bf16[64,448]{1,0:T(8,128)(2,1)}, u32[]{:S(2)}) %copy-start.2) | copy-done | bytes 57368
  3.0 0.0 copy-start.3
  3.0 0.7 copy-done.3
  3.7 0.0 copy-start.4
  3.7 0.7 copy-done.4
  4.4 73.3 %shard_map.64 = f32[8,1024]{1,0:T(8,128)S(1)} custom-call(bf16[128,14336]{1,0:T(8,128)(2,1)} %acts_hbm.1, bf16[128,4096]{1,0:T(8,128)(2,1)S(1)} %copy-done, bf16[64,448]{1,0:T(8,128)(2,1)S(1)} %copy-done.2, bf16[64,128]{1,0:T(8,128)(2,1)S(1)} %copy-done.3, s32[8]{0:T(128)S(1)} %copy-done.4, bf16[32,4096]{1,0:T(8,128)(2,1)S(1)} %copy-done.1), custom_call_target="tpu_custom_call" | custom-call | tf_op jit(solution)/shard_map/pallas_call | solution.py:362
  77.7 0.6 copy.8
Async XLA Ops:
  0.0 1.2 %copy-start = (bf16[128,4096]{1,0:T(8,128)(2,1)S(1)}, bf16[128,4096]{1,0:T(8,128)(2,1)}, u32[]{:S(2)}) copy-start(bf16[128,4096]{1,0:T(8,128)(2,1)} %outg_hbm.1) | copy-start | bytes 3145732
  1.2 0.9 %copy-start.1 = (bf16[32,4096]{1,0:T(8,128)(2,1)S(1)}, bf16[32,4096]{1,0:T(8,128)(2,1)}, u32[]{:S(2)}) copy-start(bf16[32,4096]{1,0:T(8,128)(2,1)} %q_hbm.1) | copy-start | bytes 786436
  2.2 0.8 %copy-start.2 = (bf16[64,448]{1,0:T(8,128)(2,1)S(1)}, bf16[64,448]{1,0:T(8,128)(2,1)}, u32[]{:S(2)}) copy-start(bf16[64,448]{1,0:T(8,128)(2,1)} %inp_ref.1) | copy-start | bytes 172036
  3.0 0.7 copy-start.3
  3.7 0.7 copy-start.4

commit v2 on v1

v2 whole, which is shorter than its diff:
```python
import functools
import heapq

import jax
import jax.numpy as jnp
from jax import lax
from jax.experimental import pallas as pl
from jax.experimental.pallas import tpu as pltpu
from jax.sharding import PartitionSpec as P

MESH = pl.DeviceIdType.MESH
RANK = 64
SEQ = 16
TOK = 128
IN_COLS = 448
IN_PAD = 512
OUT_COLS = 128
BLK = IN_PAD + OUT_COLS
Q_ROWS = 32
NT = (((1,), (1,)), ((), ()))
NN = (((1,), (0,)), ((), ()))
HIGHEST = lax.Precision.HIGHEST


def dot(a, b, dims=NN, precision=None):
    return lax.dot_general(a, b, dims, precision=precision, preferred_element_type=jnp.float32)


def split(x):
    hi = x.astype(jnp.bfloat16)
    return hi, (x - hi.astype(jnp.float32)).astype(jnp.bfloat16)


def damped_inverses(total, tokens):
    lane = lax.broadcasted_iota(jnp.int32, (RANK, TOK), 1)
    row = lax.broadcasted_iota(jnp.int32, (RANK, TOK), 0)
    mean = total * (1.0 / tokens)
    done = []
    for work in (mean, pltpu.roll(mean, RANK, 1)):
        diagonal = row == lane
        trace = jnp.sum(jnp.where(diagonal, work, 0.0))
        work = jnp.where(lane < RANK, work, 0.0)
        done.append(jnp.where(diagonal, work + 0.1 * trace / RANK, work))
    one, two = done
    lane1 = lax.broadcasted_iota(jnp.int32, (1, TOK), 1)
    for k in range(RANK):
        new = []
        for work in (one, two):
            pivot_row = work[k : k + 1, :]
            inverse = 1.0 / pivot_row[:, k : k + 1]
            scaled = jnp.where(lane1 == k, inverse, pivot_row * inverse)
            update = jnp.where(lane == k, 0.0, work) - work[:, k : k + 1] * scaled
            new.append(jnp.where(row == k, scaled, update))
        one, two = new
    return one, two


def gather_order(Z):
    H = Z // 2
    latency, send_time, lag = 2.3, 0.8, 0.6
    free, heap, order, held = {}, [], [], {}

    def send(t, link, event):
        start = max(t, free.get(link, 0.0))
        free[link] = start + send_time
        heapq.heappush(heap, (start + send_time + latency, len(free) + len(order), len(heap), event))

    def arrived(t, kind, way, dist, part):
        order.append((t, len(order), (kind, way, dist, part)))
        if kind == "z":
            for to in (0, 1) if dist == 0 else (way,):
                if goes_on(H, dist, to, part):
                    send(t, to, ("z", to, dist + 1, part))
            if part == 0:
                send(t, "c", ("c", way, dist, part))
        elif kind == "c":
            send(t, "p", ("p", way, dist, part))
        name = (kind != "z", 0 if dist == H else way, dist)
        held[name] = held.get(name, 0) + 1
        if held[name] == 2:
            order.append((t + lag, len(order), ("fold",) + name))

    arrived(0.0, "z", 0, 0, 0)
    arrived(0.0, "z", 0, 0, 1)
    while heap:
        t, _, _, event = heapq.heappop(heap)
        arrived(t, *event)
    return [event for _, _, event in sorted(order)]


def goes_on(H, dist, way, part):
    return dist + 1 < H or (dist + 1 == H and part == way)


def kernel(
    Y, Z, tokens,
    acts_hbm, outg_hbm, inp_hbm, outp_hbm, len_hbm, q_hbm,
    out_ref,
    acts, outg, inp, outp, lens, qraw, stage, gath, halves, other, qall, tok, part, total, ar1, ar2, ar3, mine, gsc, sco, ret,
    loc_sem, act_loc, act_send, act_recv, og_sem, z_send, z_recv, cx_send, cx_recv, pt_send, pt_recv, sw_sem,
    t_send, t_recv, q_send, q_recv, a_send, a_recv,
):
    H = Z // 2
    dpi, qi = lax.axis_index("dp"), lax.axis_index("query")
    y, xl = dpi // 2, dpi % 2
    xh, z, c = qi // (2 * Z), (qi // 2) % Z, qi % 2

    def at(y_, xl_, xh_, z_, c_):
        return (y_ * 2 + xl_, xh_ * (2 * Z) + z_ * 2 + c_)

    def zp(off):
        return (z + (off + Z)) % Z

    def z_peer(off):
        return at(y, xl, xh, zp(off), c)

    def y_peer(off):
        return at((y + off) % Y, xl, xh, z, c)

    def x_peer(m):
        return at(y, (xl + (m // 2) % 2) % 2, (xh + m // 4) % 2, z, (c + m % 2) % 2)

    cross = at(y, 1 - xl, 1 - xh, z, c)
    partner = at(y, 1 - xl, xh, z, c)
    sibling = at(y, xl, xh, z, 1 - c)

    pending = []

    def push(ref_src, ref_dst, send, recv, to):
        copy = pltpu.make_async_remote_copy(
            src_ref=ref_src, dst_ref=ref_dst, send_sem=send, recv_sem=recv, device_id=to, device_id_type=MESH
        )
        copy.start()
        pending.append(copy)

    def got(ref, sem):
        pltpu.make_async_copy(ref, ref, sem).wait()

    barrier = pltpu.get_barrier_semaphore()
    peers = [z_peer(d) for d in range(1, Z)] + [x_peer(m) for m in range(1, 8)] + [y_peer(d) for d in range(1, Y)]
    for peer in peers:
        pl.semaphore_signal(barrier, inc=1, device_id=peer, device_id_type=MESH)

    loads = [
        pltpu.make_async_copy(inp_hbm, inp, loc_sem.at[0]),
        pltpu.make_async_copy(outp_hbm, outp, loc_sem.at[1]),
        pltpu.make_async_copy(q_hbm, qraw, loc_sem.at[2]),
        pltpu.make_async_copy(len_hbm, lens, loc_sem.at[3]),
    ]
    for load in loads:
        load.start()

    order = gather_order(Z)
    folds = [event for event in order if event[0] == "fold"]

    def off_of(way, dist):
        return dist if way == 1 else -dist

    def window(far, way, dist):
        return ((1 - xh) if far else xh) * Z + zp(off_of(way, dist))

    def act_columns(k, cc):
        return pl.ds(pl.multiple_of(k * (2 * IN_COLS) + cc * (IN_COLS - RANK), 128), IN_PAD)

    def act_slot(k, cc):
        return acts.at[pl.ds(pl.multiple_of(cc * TOK, TOK), TOK), pl.ds(pl.multiple_of(k * IN_PAD, IN_PAD), IN_PAD)]

    def out_slot(cc):
        return outg.at[pl.ds(pl.multiple_of(cc * TOK, TOK), TOK), :]

    own_loads = []
    for j, (_, far, way, dist) in enumerate(folds):
        k = window(far, way, dist)
        own_loads.append(pltpu.make_async_copy(acts_hbm.at[:, act_columns(k, c)], act_slot(k, c), act_loc.at[j]))
        own_loads[-1].start()
        if j == 0:
            out_load = pltpu.make_async_copy(outg_hbm, out_slot(c), og_sem.at[0])
            out_load.start()

    def piece(h, zz, p):
        return gath.at[pl.ds(pl.multiple_of((h * Z + zz) * RANK + p * 32, 32), 32), :]

    stage[...] = jnp.zeros_like(stage)
    loads[0].wait()
    loads[1].wait()
    stage[:, 0:IN_COLS] = inp[...].astype(jnp.float32)
    plain = stage[...]
    shifted = pltpu.roll(plain, IN_PAD - IN_COLS, 1)
    own_rows = pl.ds(pl.multiple_of((xh * Z + z) * RANK, RANK), RANK)
    gath[own_rows, 0:IN_PAD] = jnp.where(c == 1, shifted, plain).astype(jnp.bfloat16)
    gath[own_rows, IN_PAD:BLK] = outp[...]
    pl.semaphore_wait(barrier, len(peers))

    lane_q = lax.broadcasted_iota(jnp.int32, (Q_ROWS, TOK), 1)
    q_cols = qraw.shape[1]

    def q_slot(h, cc):
        return (h * 2 + cc) * Q_ROWS

    def q_piece(h, cc, p):
        half = Q_ROWS // 2
        return qall.at[pl.ds(pl.multiple_of(q_slot(h, cc) + p * half, half), half), :]

    own_q = pl.ds(pl.multiple_of(q_slot(xh, c), Q_ROWS), Q_ROWS)

    def pair_queries():
        loads[2].wait()
        for m in range(q_cols // 256):
            first = qraw[:, 128 * m : 128 * m + 128].astype(jnp.float32)
            second = qraw[:, q_cols // 2 + 128 * m : q_cols // 2 + 128 * m + 128].astype(jnp.float32)
            low = jnp.where(lane_q < RANK, first, pltpu.roll(second, RANK, 1))
            high = jnp.where(lane_q < RANK, pltpu.roll(first, RANK, 1), second)
            qall[own_q, 256 * m : 256 * m + 128] = low.astype(jnp.bfloat16)
            qall[own_q, 256 * m + 128 : 256 * m + 256] = high.astype(jnp.bfloat16)

    sums = [jnp.zeros((RANK, 2 * TOK), jnp.float32), jnp.zeros((RANK, 2 * TOK), jnp.float32)]
    first_fold = True
    for event in order:
        kind, rest = event[0], event[1:]
        if kind == "z":
            way, dist, p = rest
            ref = piece(xh, zp(off_of(way, dist)), xl if p == 0 else 1 - xl)
            if dist > 0:
                got(ref, z_recv.at[way, dist - 1, p])
            for to in (0, 1) if dist == 0 else (way,):
                if goes_on(H, dist, to, p):
                    push(ref, ref, z_send.at[to, dist, p], z_recv.at[to, dist, p], z_peer(1 if to == 0 else -1))
            if p == 0:
                push(ref, ref, cx_send.at[way, dist], cx_recv.at[way, dist], cross)
        elif kind == "c":
            way, dist, _ = rest
            ref = piece(1 - xh, zp(off_of(way, dist)), 1 - xl)
            got(ref, cx_recv.at[way, dist])
            push(ref, ref, pt_send.at[way, dist], pt_recv.at[way, dist], partner)
        elif kind == "p":
            way, dist, _ = rest
            got(piece(1 - xh, zp(off_of(way, dist)), xl), pt_recv.at[way, dist])
        else:
            far, way, dist = rest
            if first_fold:
                first_fold = False
                for j, (_, far_, way_, dist_) in enumerate(folds):
                    k = window(far_, way_, dist_)
                    push(acts_hbm.at[:, act_columns(k, 1 - c)], act_slot(k, c), act_send.at[j], act_recv.at[j], sibling)
                    if j == 0:
                        push(outg_hbm, out_slot(c), og_sem.at[1], og_sem.at[2], sibling)
                pair_queries()
                out_load.wait()
                got(out_slot(1 - c), og_sem.at[2])
            j = folds.index(event)
            k = window(far, way, dist)
            own_loads[j].wait()
            got(act_slot(k, 1 - c), act_recv.at[j])
            rows = pl.ds(pl.multiple_of(k * RANK, RANK), RANK)
            columns = pl.ds(pl.multiple_of(k * IN_PAD, IN_PAD), IN_PAD)
            sums[0] = sums[0] + dot(gath[rows, 0:IN_PAD], acts[:, columns], NT)
            columns = pl.ds(pl.multiple_of(k * (2 * OUT_COLS) + c * OUT_COLS, OUT_COLS), OUT_COLS)
            sums[1] = sums[1] + dot(gath[rows, IN_PAD:BLK], outg[:, columns], NT)

    ref = q_piece(xh, c, xl)
    push(ref, ref, q_send.at[0], q_recv.at[0], cross)
    for cc in range(2):
        halves[cc] = jnp.concatenate([sums[0][:, cc * TOK : (cc + 1) * TOK], sums[1][:, cc * TOK : (cc + 1) * TOK]], axis=0)
    push(halves.at[1 - c], other, sw_sem.at[0], sw_sem.at[1], sibling)
    ref = qall.at[own_q, :]
    push(ref, ref, q_send.at[1], q_recv.at[1], sibling)

    lane1 = lax.broadcasted_iota(jnp.int32, (1, TOK), 1)
    counts = jnp.zeros((1, TOK), jnp.int32)
    loads[3].wait()
    for e in range(TOK // SEQ):
        counts = jnp.where(lane1 // SEQ == e, lens[e], counts)
    live = (lane1 % SEQ < counts).astype(jnp.float32)
    got(other, sw_sem.at[1])
    masked = (halves[c] + other[...]) * live
    own_tok = pl.ds(pl.multiple_of(z * TOK, TOK), TOK)
    tok[own_tok, :] = masked
    gram = dot(masked, masked, NT, HIGHEST)
    lane = lax.broadcasted_iota(jnp.int32, (RANK, TOK), 1)
    part[...] = jnp.where(lane < RANK, gram[0:RANK], gram[RANK:])

    rows_z = RANK // Z

    def z_rows(zz):
        return pl.ds(pl.multiple_of(zz * rows_z, rows_z), rows_z)

    def tok_piece(zz, p):
        return tok.at[pl.ds(pl.multiple_of(zz * TOK + p * RANK, RANK), RANK), :]

    def tok_step(dist):
        for way, sign in ((0, -1), (1, 1)):
            for p in (0, 1):
                ref = tok_piece(zp(sign * dist), p)
                if dist == H and p != way:
                    continue
                if dist > 0:
                    got(ref, t_recv.at[way, dist - 1, p])
                if goes_on(H, dist, way, p):
                    push(ref, ref, t_send.at[way, dist, p], t_recv.at[way, dist, p], z_peer(-sign))

    for d in range(1, Z):
        push(part.at[z_rows(zp(d)), :], ar1.at[d - 1], a_send.at[0, d - 1], a_recv.at[0], z_peer(d))
    tok_step(0)
    got(ar1, a_recv.at[0])
    summed = part[z_rows(z), :]
    for d in range(Z - 1):
        summed = summed + ar1[d]
    mine[0] = summed
    for d in range(1, Y):
        push(mine.at[0], ar2.at[d - 1], a_send.at[1, d - 1], a_recv.at[1], y_peer(d))
    tok_step(1)
    ref = q_piece(1 - xh, c, 1 - xl)
    got(ref, q_recv.at[0])
    push(ref, ref, q_send.at[2], q_recv.at[2], partner)
    push(ref, ref, q_send.at[3], q_recv.at[3], sibling)
    got(ar2, a_recv.at[1])
    for d in range(Y - 1):
        summed = summed + ar2[d]
    mine[1] = summed
    for m in range(1, 8):
        push(mine.at[1], ar3.at[m - 1], a_send.at[2, m - 1], a_recv.at[2], x_peer(m))
    if H > 2:
        tok_step(2)
    got(ar3, a_recv.at[2])
    for m in range(7):
        summed = summed + ar3[m]
    total[z_rows(z), :] = summed
    for d in range(1, Z):
        here = total.at[z_rows(z), :]
        push(here, here, a_send.at[3, d - 1], a_recv.at[3], z_peer(d))
    if H > 3:
        tok_step(3)
    ref = q_piece(1 - xh, c, xl)
    got(ref, q_recv.at[2])
    push(ref, ref, q_send.at[4], q_recv.at[4], sibling)
    got(total.at[0 : RANK - rows_z, :], a_recv.at[3])

    in_inverse, out_inverse = damped_inverses(total[...], tokens)

    if H > 1:
        tok_step(H)

    example = lax.broadcasted_iota(jnp.int32, (SEQ // 2, TOK), 0)
    token = lax.broadcasted_iota(jnp.int32, (SEQ // 2, TOK), 1)
    belongs = (token // SEQ == example).astype(jnp.float32)
    nothing = jnp.zeros((RANK, TOK), jnp.bfloat16)
    half = RANK // 2
    for k in range(Z):
        ins = dot(in_inverse[:, 0:RANK], tok[k * TOK : k * TOK + RANK, :], NN, HIGHEST)
        outs = dot(out_inverse[:, 0:RANK], tok[k * TOK + RANK : (k + 1) * TOK, :], NN, HIGHEST)
        left, right = [], []
        for w in split(outs):
            spread = (w.astype(jnp.float32)[:, None, :] * belongs[None, :, :]).astype(jnp.bfloat16)
            spread = spread.reshape(RANK * 8, TOK)
            left.append(jnp.concatenate([spread[0 : half * 8], spread[half * 8 :]], axis=1))
        for w in split(ins):
            right.append(
                jnp.concatenate(
                    [jnp.concatenate([w, nothing], axis=1), jnp.concatenate([nothing, w], axis=1)], axis=0
                )
            )
        grads = dot(left[0], right[0], NT) + (dot(left[0], right[1], NT) + dot(left[1], right[0], NT))
        gsc[:, k * 8 : (k + 1) * 8, :] = grads.reshape(half, 8, TOK)

    got(qall.at[pl.ds(pl.multiple_of(q_slot(xh, 1 - c), Q_ROWS), Q_ROWS), :], q_recv.at[1])
    got(q_piece(1 - xh, 1 - c, 1 - xl), q_recv.at[3])
    got(q_piece(1 - xh, 1 - c, xl), q_recv.at[4])
    scores = jnp.zeros((2 * 8 * Z, TOK), jnp.float32)
    for m in range(half // 2):
        both = jnp.concatenate([gsc[2 * m], gsc[2 * m + 1]], axis=1)
        hi, lo = split(both)
        scores = scores + dot(jnp.concatenate([hi, lo], axis=0), qall[:, 256 * m : 256 * m + 256], NT)
    sco[...] = scores[0 : 8 * Z] + scores[8 * Z :]
    for d in range(1, Z):
        push(
            sco.at[pl.ds(pl.multiple_of(zp(d) * 8, 8), 8), :], ret.at[d], a_send.at[4, d - 1], a_recv.at[4], z_peer(d)
        )
    ret[0] = sco[pl.ds(pl.multiple_of(z * 8, 8), 8), :]
    got(ret.at[1:Z], a_recv.at[4])
    lane8 = lax.broadcasted_iota(jnp.int32, (8, TOK), 1)
    width = Z * RANK
    for m in range(Z // 2):
        first = ret[zp(-2 * m)]
        second = ret[zp(-2 * m - 1)]
        out_ref[:, 128 * m : 128 * m + 128] = jnp.where(lane8 < RANK, first, pltpu.roll(second, RANK, 1))
        out_ref[:, width + 128 * m : width + 128 * m + 128] = jnp.where(
            lane8 < RANK, pltpu.roll(first, RANK, 1), second
        )
    for copy in pending:
        copy.wait_send()


def solution(mesh):
    Y, Z = mesh.shape["dp"] // 2, mesh.shape["query"] // 4
    H = Z // 2

    def on_device(activations, out_grads, in_projection, out_projection, lengths, queries):
        tokens = activations.shape[0] * mesh.shape["dp"] * mesh.shape["query"]
        f32, bf16 = jnp.float32, jnp.bfloat16
        sem = pltpu.SemaphoreType.DMA
        return pl.pallas_call(
            functools.partial(kernel, Y, Z, tokens),
            out_shape=jax.ShapeDtypeStruct((lengths.shape[0], Z * 4 * Q_ROWS), f32),
            in_specs=[pl.BlockSpec(memory_space=pltpu.HBM)] * 6,
            out_specs=pl.BlockSpec(memory_space=pltpu.VMEM),
            scratch_shapes=[
                pltpu.VMEM((2 * TOK, 2 * Z * IN_PAD), bf16),
                pltpu.VMEM((2 * TOK, out_grads.shape[1]), bf16),
                pltpu.VMEM(in_projection.shape, bf16),
                pltpu.VMEM(out_projection.shape, bf16),
                pltpu.SMEM(lengths.shape, jnp.int32),
                pltpu.VMEM(queries.shape, bf16),
                pltpu.VMEM((RANK, IN_PAD), f32),
                pltpu.VMEM((2 * Z * RANK, BLK), bf16),
                pltpu.VMEM((2, TOK, TOK), f32),
                pltpu.VMEM((TOK, TOK), f32),
                pltpu.VMEM((4 * Q_ROWS, queries.shape[1]), bf16),
                pltpu.VMEM((Z * TOK, TOK), f32),
                pltpu.VMEM((RANK, TOK), f32),
                pltpu.VMEM((RANK, TOK), f32),
                pltpu.VMEM((Z - 1, RANK // Z, TOK), f32),
                pltpu.VMEM((Y - 1, RANK // Z, TOK), f32),
                pltpu.VMEM((7, RANK // Z, TOK), f32),
                pltpu.VMEM((2, RANK // Z, TOK), f32),
                pltpu.VMEM((RANK // 2, 8 * Z, TOK), f32),
                pltpu.VMEM((8 * Z, TOK), f32),
                pltpu.VMEM((Z, 8, TOK), f32),
                sem((4,)),
                sem((2 * Z,)),
                sem((2 * Z,)),
                sem((2 * Z,)),
                sem((3,)),
                sem((2, H, 2)),
                sem((2, H, 2)),
                sem((2, H + 1)),
                sem((2, H + 1)),
                sem((2, H + 1)),
                sem((2, H + 1)),
                sem((2,)),
                sem((2, H, 2)),
                sem((2, H, 2)),
                sem((5,)),
                sem((5,)),
                sem((5, 7)),
                sem((5,)),
            ],
            compiler_params=pltpu.CompilerParams(
                collective_id=0, has_side_effects=True, vmem_limit_bytes=60 * 1024 * 1024
            ),
        )(activations, out_grads, in_projection, out_projection, lengths, queries)

    placed = (
        P(("dp", "query"), None),
        P(("dp", "query"), None),
        P(None, "query"),
        P(None, "query"),
        P(("dp", "query")),
        P("query", None),
    )
    return jax.shard_map(
        on_device, mesh=mesh, in_specs=placed, out_specs=P(("dp", "query"), None), check_vma=False
    )
```

time: 79.5 us -> 69.7 us (0.88)
  Pallas kernels: 73.3 us -> 67.8 us
  local copies, waits for them, and re-layouts: 5 us -> 1.38 us
    pallas_call x1, Pallas kernels: 73.3 us -> 67.8 us  [on_device(): pl.pallas_call(functools.partial(kernel, Y, Z, tokens), out_shape=jax.Sha...]
    unnamed x11 -> x1, local copies, waits for them, and re-layouts: 5 us -> 1.38 us
where the time goes in v2:
time: 69.7 us; the launch traced here: 69.2 us
  Pallas kernels  67.8 us (97%)
  local copies, waits for them, and re-layouts  1.38 us (2%)
    pallas_call x1, Pallas kernels, on_device(): pl.pallas_call(functools.partial(kernel, Y, Z, tokens), out_shape=jax.Sha...  67.8 us

profile of v2, /device:TPU:1, one launch (start us, length us, event | category | flops | bytes accessed | tf_op | source)
XLA Modules:
  0.0 69.2 jit_solution(7077008290930233578)
XLA Ops:
  0.0 67.8 %shard_map.64 = f32[8,1024]{1,0:T(8,128)} custom-call(bf16[128,14336]{1,0:T(8,128)(2,1)} %acts_hbm.1, bf16[128,4096]{1,0:T(8,128)(2,1)} %outg_hbm.1, bf16[64,448]{1,0:T(8,128)(2,1)} %inp_hbm.1, bf16[64,128]{1,0:T(8,128)(2,1)} %outp_hbm.1, s32[8]{0:T(128)} %len_hbm.1, bf16[32,4096]{1,0:T(8,128)(2,1)} %q_hbm.1), custom_call_target="tpu_custom_call" | custom-call | tf_op jit(solution)/shard_map/pallas_call | solution.py:401
  67.8 1.4 %copy.8 = f32[8,1024]{1,0:T(8,128)} copy(f32[8,1024]{1,0:T(8,128)} %shard_map.64) | data formatting | bytes 65536

commit v3 on v2

v3 whole, which is shorter than its diff:
```python
import functools

import jax
import jax.numpy as jnp
from jax import lax
from jax.experimental import pallas as pl
from jax.experimental.pallas import tpu as pltpu
from jax.sharding import PartitionSpec as P

MESH = pl.DeviceIdType.MESH
RANK = 64
SEQ = 16
TOK = 128
IN_COLS = 448
IN_PAD = 512
OUT_COLS = 128
BLK = IN_PAD + OUT_COLS
Q_ROWS = 32
NT = (((1,), (1,)), ((), ()))
NN = (((1,), (0,)), ((), ()))


def dot(a, b, dims=NN):
    return lax.dot_general(a, b, dims, preferred_element_type=jnp.float32)


def split(x):
    hi = x.astype(jnp.bfloat16)
    return hi, (x - hi.astype(jnp.float32)).astype(jnp.bfloat16)


def inverse_of_four(p):
    a, b, d = p[0][0], p[0][1], p[1][1]
    scale = 1.0 / (a * d - b * b)
    u00, u01, u11 = d * scale, -b * scale, a * scale
    c = [[p[0][2], p[0][3]], [p[1][2], p[1][3]]]
    x = [[u00 * c[0][j] + u01 * c[1][j] for j in range(2)], [u01 * c[0][j] + u11 * c[1][j] for j in range(2)]]
    s00 = p[2][2] - (c[0][0] * x[0][0] + c[1][0] * x[1][0])
    s01 = p[2][3] - (c[0][0] * x[0][1] + c[1][0] * x[1][1])
    s11 = p[3][3] - (c[0][1] * x[0][1] + c[1][1] * x[1][1])
    scale = 1.0 / (s00 * s11 - s01 * s01)
    t00, t01, t11 = s11 * scale, -s01 * scale, s00 * scale
    w = [[x[i][0] * t00 + x[i][1] * t01, x[i][0] * t01 + x[i][1] * t11] for i in range(2)]
    v00 = u00 + w[0][0] * x[0][0] + w[0][1] * x[0][1]
    v01 = u01 + w[0][0] * x[1][0] + w[0][1] * x[1][1]
    v11 = u11 + w[1][0] * x[1][0] + w[1][1] * x[1][1]
    return [
        [v00, v01, -w[0][0], -w[0][1]],
        [v01, v11, -w[1][0], -w[1][1]],
        [-w[0][0], -w[1][0], t00, t01],
        [-w[0][1], -w[1][1], t01, t11],
    ]


def damped_inverses(total, tokens):
    lane = lax.broadcasted_iota(jnp.int32, (RANK, TOK), 1)
    row = lax.broadcasted_iota(jnp.int32, (RANK, TOK), 0)
    column = lane % RANK
    left = lane < RANK
    work = total * (1.0 / tokens)
    diagonal = jnp.where(column == row, work, 0.0)
    trace = jnp.where(left, jnp.sum(jnp.where(left, diagonal, 0.0)), jnp.sum(jnp.where(left, 0.0, diagonal)))
    work = jnp.where(column == row, work + 0.1 * trace / RANK, work)
    first = jnp.where(left, 0, RANK)
    column1 = lax.broadcasted_iota(jnp.int32, (1, TOK), 1) % RANK
    for k in range(0, RANK, 4):
        columns = [jnp.take_along_axis(work, first + (k + i), axis=1) for i in range(4)]
        rows = [work[k + i : k + i + 1] for i in range(4)]
        pivot = inverse_of_four([[columns[j][k + i : k + i + 1] for j in range(4)] for i in range(4)])
        scaled = []
        for i in range(4):
            value = (pivot[i][0] * rows[0] + pivot[i][1] * rows[1]) + (pivot[i][2] * rows[2] + pivot[i][3] * rows[3])
            for j in range(4):
                value = jnp.where(column1 == k + j, pivot[i][j], value)
            scaled.append(value)
        work = jnp.where((column >= k) & (column < k + 4), 0.0, work)
        work = (work - columns[0] * scaled[0] - columns[1] * scaled[1]) - (
            columns[2] * scaled[2] + columns[3] * scaled[3]
        )
        for i in range(4):
            work = jnp.where(row == k + i, scaled[i], work)
    return work


def gather_order(Z):
    H = Z // 2
    times = {d: 4.5 + 0.95 * (H - 1 - d) for d in range(1, H)}
    times[H] = max(times.get(H - 1, 4.5) + 2.5, 7.0)
    order = [(0.3, "near", 0), (5.0, "q", 0), (9.4, "q", 1)]
    for off in [0] + [sign * d for d in range(H - 1, 0, -1) for sign in (-1, 1)] + [H]:
        t = times[abs(off)] if off else 0.0
        if off:
            order += [(t, "z", off), (t + 2.7, "y", off), (t + 2.75, "near", off)]
        order += [(t + 2.7, "c", off), (t + 5.2, "p", off), (t + 5.3, "far", off)]
    return [event[1:] for event in sorted(order, key=lambda event: event[0])]


def goes_on(H, dist, way, part):
    return dist + 1 < H or (dist + 1 == H and part == way)


def kernel(
    Y, Z, tokens,
    acts_hbm, outg_hbm, inp_hbm, outp_hbm, len_hbm, q_hbm,
    out_ref,
    acts, outg, inp, outp, lens, qraw, stage, gath, halves, other, both, spare, lives, qall, tok, part, total, ar1, ar2, ar3, mine, gsc, sco, ret,
    loc_sem, act_loc, act_send, act_recv, og_sem, z_send, z_recv, r_send, r_recv, y_send, y_recv, cx_send, cx_recv,
    pt_send, pt_recv, sw_sem,
    t_send, t_recv, q_send, q_recv, a_send, a_recv,
):
    H = Z // 2
    dpi, qi = lax.axis_index("dp"), lax.axis_index("query")
    y, xl = dpi // 2, dpi % 2
    xh, z, c = qi // (2 * Z), (qi // 2) % Z, qi % 2

    def at(y_, xl_, xh_, z_, c_):
        return (y_ * 2 + xl_, xh_ * (2 * Z) + z_ * 2 + c_)

    def zp(off):
        return (z + (off + Z)) % Z

    def z_peer(off):
        return at(y, xl, xh, zp(off), c)

    def y_peer(off):
        return at((y + off) % Y, xl, xh, z, c)

    def x_peer(m):
        return at(y, (xl + (m // 2) % 2) % 2, (xh + m // 4) % 2, z, (c + m % 2) % 2)

    cross = at(y, 1 - xl, 1 - xh, z, c)
    partner = at(y, 1 - xl, xh, z, c)
    sibling = at(y, xl, xh, z, 1 - c)

    pending = []

    def push(ref_src, ref_dst, send, recv, to):
        copy = pltpu.make_async_remote_copy(
            src_ref=ref_src, dst_ref=ref_dst, send_sem=send, recv_sem=recv, device_id=to, device_id_type=MESH
        )
        copy.start()
        pending.append(copy)

    def got(ref, sem):
        pltpu.make_async_copy(ref, ref, sem).wait()

    loads = [
        pltpu.make_async_copy(inp_hbm, inp, loc_sem.at[0]),
        pltpu.make_async_copy(outp_hbm, outp, loc_sem.at[1]),
        pltpu.make_async_copy(q_hbm, qraw, loc_sem.at[2]),
        pltpu.make_async_copy(len_hbm, lens, loc_sem.at[3]),
    ]
    for load in loads:
        load.start()

    barrier = pltpu.get_barrier_semaphore()
    peers = [y_peer(d) for d in range(1, Y)] + [z_peer(d) for d in range(1, Z)] + [x_peer(m) for m in range(7, 0, -1)]
    for peer in peers:
        pl.semaphore_signal(barrier, inc=1, device_id=peer, device_id_type=MESH)

    order = gather_order(Z)
    folds = [event for event in order if event[0] in ("near", "far")]

    def window(name, off):
        return (xh if name == "near" else 1 - xh) * Z + zp(off)

    def act_columns(k, cc):
        return pl.ds(pl.multiple_of(k * (2 * IN_COLS) + cc * (IN_COLS - RANK), 128), IN_PAD)

    def act_slot(k, cc):
        return acts.at[pl.ds(pl.multiple_of(cc * TOK, TOK), TOK), pl.ds(pl.multiple_of(k * IN_PAD, IN_PAD), IN_PAD)]

    def out_slot(cc):
        return outg.at[pl.ds(pl.multiple_of(cc * TOK, TOK), TOK), :]

    mate = at(y + 1 - 2 * (y % 2), xl, xh, z, c)
    side = (y + xl) % 2

    def piece(h, off, p):
        return gath.at[pl.ds(pl.multiple_of((h * Z + zp(off)) * RANK + p * 32, 32), 32), :]

    def quarter(off, r):
        return gath.at[pl.ds(pl.multiple_of((xh * Z + zp(off)) * RANK + side * 32 + r * 16, 16), 16), :]

    stage[...] = jnp.zeros_like(stage)
    loads[0].wait()
    loads[1].wait()
    stage[:, 0:IN_COLS] = inp[...].astype(jnp.float32)
    plain = stage[...]
    shifted = pltpu.roll(plain, IN_PAD - IN_COLS, 1)
    own_rows = pl.ds(pl.multiple_of((xh * Z + z) * RANK, RANK), RANK)
    gath[own_rows, 0:IN_PAD] = jnp.where(c == 1, shifted, plain).astype(jnp.bfloat16)
    gath[own_rows, IN_PAD:BLK] = outp[...]
    pl.semaphore_wait(barrier, len(peers))

    lane_q = lax.broadcasted_iota(jnp.int32, (Q_ROWS, TOK), 1)
    q_cols = qraw.shape[1]

    def q_slot(h, cc):
        return (h * 2 + cc) * Q_ROWS

    def q_piece(h, cc, p):
        half = Q_ROWS // 2
        return qall.at[pl.ds(pl.multiple_of(q_slot(h, cc) + p * half, half), half), :]

    own_q = pl.ds(pl.multiple_of(q_slot(xh, c), Q_ROWS), Q_ROWS)

    def pair_queries():
        loads[2].wait()
        for m in range(q_cols // 256):
            first = qraw[:, 128 * m : 128 * m + 128].astype(jnp.float32)
            second = qraw[:, q_cols // 2 + 128 * m : q_cols // 2 + 128 * m + 128].astype(jnp.float32)
            low = jnp.where(lane_q < RANK, first, pltpu.roll(second, RANK, 1))
            high = jnp.where(lane_q < RANK, pltpu.roll(first, RANK, 1), second)
            qall[own_q, 256 * m : 256 * m + 128] = low.astype(jnp.bfloat16)
            qall[own_q, 256 * m + 128 : 256 * m + 256] = high.astype(jnp.bfloat16)

    sums = [jnp.zeros((RANK, 2 * TOK), jnp.float32), jnp.zeros((RANK, 2 * TOK), jnp.float32)]
    ref = piece(xh, 0, side)
    for d in range(H - 1, 0, -1):
        for sign in (1, -1):
            push(ref, ref, z_send.at[H - 1 + sign * d], z_recv.at[H - 1 - sign * d], z_peer(sign * d))
    push(ref, ref, cx_send.at[H - 1], cx_recv.at[H - 1], cross)
    own_loads = []
    for j, fold in enumerate(folds):
        k = window(*fold)
        own_loads.append(pltpu.make_async_copy(acts_hbm.at[:, act_columns(k, c)], act_slot(k, c), act_loc.at[j]))
        own_loads[-1].start()
        if j == 0:
            out_load = pltpu.make_async_copy(outg_hbm, out_slot(c), og_sem.at[0])
            out_load.start()
    for event in order:
        kind, off = event
        slot = H - 1 + off
        if kind == "z":
            ref = piece(xh, off, side)
            if off == H:
                got(quarter(H, 0), r_recv.at[0])
                got(quarter(H, 1), r_recv.at[1])
            else:
                got(ref, z_recv.at[slot])
            for r, sign in ((0, 1), (1, -1)):
                if off == -sign * (H - 1):
                    relay = quarter(off, r)
                    push(relay, relay, r_send.at[r], r_recv.at[r], z_peer(sign))
            push(ref, ref, cx_send.at[slot], cx_recv.at[slot], cross)
            push(ref, ref, y_send.at[slot], y_recv.at[slot], mate)
        elif kind == "y":
            got(piece(xh, off, 1 - side), y_recv.at[slot])
        elif kind == "c":
            ref = piece(1 - xh, off, 1 - side)
            got(ref, cx_recv.at[slot])
            push(ref, ref, pt_send.at[slot], pt_recv.at[slot], partner)
        elif kind == "p":
            got(piece(1 - xh, off, side), pt_recv.at[slot])
        elif event == ("q", 0):
            ref = q_piece(1 - xh, c, 1 - xl)
            got(ref, q_recv.at[0])
            push(ref, ref, q_send.at[2], q_recv.at[2], partner)
            push(ref, ref, q_send.at[3], q_recv.at[3], sibling)
        elif event == ("q", 1):
            ref = q_piece(1 - xh, c, xl)
            got(ref, q_recv.at[2])
            push(ref, ref, q_send.at[4], q_recv.at[4], sibling)
        else:
            j = folds.index(event)
            if j == 0:
                for i, fold in enumerate(folds):
                    k = window(*fold)
                    push(acts_hbm.at[:, act_columns(k, 1 - c)], act_slot(k, c), act_send.at[i], act_recv.at[i], sibling)
                    if i == 0:
                        push(outg_hbm, out_slot(c), og_sem.at[1], og_sem.at[2], sibling)
                pair_queries()
                ref = q_piece(xh, c, xl)
                push(ref, ref, q_send.at[0], q_recv.at[0], cross)
                ref = qall.at[own_q, :]
                push(ref, ref, q_send.at[1], q_recv.at[1], sibling)
                lane1 = lax.broadcasted_iota(jnp.int32, (8, TOK), 1)
                counts = jnp.zeros((8, TOK), jnp.int32)
                loads[3].wait()
                for e in range(TOK // SEQ):
                    counts = jnp.where(lane1 // SEQ == e, lens[e], counts)
                lives[c] = (lane1 % SEQ < counts).astype(jnp.float32)
                push(lives.at[c], lives.at[c], sw_sem.at[2], sw_sem.at[3], sibling)
                out_load.wait()
                got(out_slot(1 - c), og_sem.at[2])
            k = window(*event)
            own_loads[j].wait()
            got(act_slot(k, 1 - c), act_recv.at[j])
            rows = pl.ds(pl.multiple_of(k * RANK, RANK), RANK)
            columns = pl.ds(pl.multiple_of(k * IN_PAD, IN_PAD), IN_PAD)
            sums[0] = sums[0] + dot(gath[rows, 0:IN_PAD], acts[:, columns], NT)
            columns = pl.ds(pl.multiple_of(k * (2 * OUT_COLS) + c * OUT_COLS, OUT_COLS), OUT_COLS)
            sums[1] = sums[1] + dot(gath[rows, IN_PAD:BLK], outg[:, columns], NT)

    halves[0] = sums[0]
    halves[1] = sums[1]
    push(halves.at[1 - c], other, sw_sem.at[0], sw_sem.at[1], sibling)
    got(lives.at[1 - c], sw_sem.at[3])
    live = jnp.concatenate([lives[0, 0:1, :], lives[1, 0:1, :]], axis=1)
    got(other, sw_sem.at[1])
    masked = (halves[c] + other[...]) * live
    both[...] = masked
    hi, lo = split(masked)
    hi_lo = jnp.concatenate([hi, lo], axis=1)
    twice = jnp.concatenate([hi_lo, hi_lo], axis=0)
    lo_hi = jnp.concatenate([lo, hi], axis=1)
    gram = dot(hi_lo, twice, NT) + dot(lo_hi, twice, NT)
    half = RANK // 2
    lane = lax.broadcasted_iota(jnp.int32, (half, TOK), 1)
    part[...] = jnp.where(lane < RANK, gram[0:half], gram[half:])

    rows_x = half // 4

    def x_rows(m):
        index = ((xh + m // 4) % 2) * 2 + (xl + (m // 2) % 2) % 2
        return pl.ds(pl.multiple_of(index * rows_x, rows_x), rows_x)

    def tok_piece(zz, p):
        return tok.at[pl.ds(pl.multiple_of(zz * TOK + p * RANK, RANK), RANK), :]

    def tok_step(dist):
        for way, sign in ((0, -1), (1, 1)):
            for p in (0, 1):
                ref = tok_piece(zp(sign * dist), p)
                if dist == H and p != way:
                    continue
                if dist > 0:
                    got(ref, t_recv.at[way, dist - 1, p])
                if goes_on(H, dist, way, p):
                    push(ref, ref, t_send.at[way, dist, p], t_recv.at[way, dist, p], z_peer(-sign))

    for j, m in enumerate((4, 6, 2)):
        push(part.at[x_rows(m), :], ar1.at[j], a_send.at[0, j], a_recv.at[0], x_peer(m))
    for cc in range(2):

        @pl.when(c == cc)
        def _():
            tok[pl.ds(pl.multiple_of(z * TOK + cc * RANK, RANK), RANK), :] = both[:, cc * TOK : (cc + 1) * TOK]
            spare[...] = both[:, (1 - cc) * TOK : (2 - cc) * TOK]

    push(spare, tok_piece(z, c), sw_sem.at[4], sw_sem.at[5], sibling)
    got(ar1, a_recv.at[0])
    summed = part[x_rows(0), :]
    for j in range(3):
        summed = summed + ar1[j]
    mine[0] = summed
    for d in range(1, Z):
        push(mine.at[0], ar2.at[d - 1], a_send.at[1, d - 1], a_recv.at[1], z_peer(d))
    got(tok_piece(z, 1 - c), sw_sem.at[5])
    tok_step(0)
    tok_step(1)
    got(ar2, a_recv.at[1])
    for d in range(Z - 1):
        summed = summed + ar2[d]
    mine[1] = summed
    for d in range(1, Y):
        push(mine.at[1], ar3.at[d - 1], a_send.at[2, d - 1], a_recv.at[2], y_peer(d))
    if H > 2:
        tok_step(2)
    got(ar3, a_recv.at[2])
    for d in range(Y - 1):
        summed = summed + ar3[d]

    def total_rows(cc):
        return total.at[pl.ds(pl.multiple_of((cc * 4 + xh * 2 + xl) * rows_x, rows_x), rows_x), :]

    here = total_rows(c)
    here[...] = summed
    for m in (5, 7, 4, 6, 3, 2, 1):
        push(here, here, a_send.at[3, m - 1], a_recv.at[3], x_peer(m))
    if H > 3:
        tok_step(3)
    got(total.at[0 : RANK - rows_x, :], a_recv.at[3])
    if H > 1:
        tok_step(H)

    ins, outs = total[0:half], total[half:]
    sides = jnp.concatenate(
        [
            jnp.where(lane < RANK, ins, pltpu.roll(outs, RANK, 1)),
            jnp.where(lane < RANK, pltpu.roll(ins, RANK, 1), outs),
        ],
        axis=0,
    )
    inverses = damped_inverses(sides, tokens)
    lane = lax.broadcasted_iota(jnp.int32, (RANK, TOK), 1)
    blocks = jnp.concatenate(
        [jnp.where(lane < RANK, inverses, 0.0), jnp.where(lane < RANK, 0.0, inverses)], axis=0
    )
    hi, lo = split(blocks)
    blocks = jnp.concatenate([hi, lo, hi], axis=1)
    example = lax.broadcasted_iota(jnp.int32, (SEQ // 2, TOK), 0)
    token = lax.broadcasted_iota(jnp.int32, (SEQ // 2, TOK), 1)
    belongs = (token // SEQ == example).astype(jnp.float32)
    nothing = jnp.zeros((RANK, TOK), jnp.bfloat16)
    for k in range(Z):
        if k % 2 == 0:
            rows = [split(tok[(k + i) * TOK : (k + i + 1) * TOK, :]) for i in range(2)]
            hi = jnp.concatenate([rows[0][0], rows[1][0]], axis=1)
            lo = jnp.concatenate([rows[0][1], rows[1][1]], axis=1)
            pair = dot(blocks, jnp.concatenate([hi, hi, lo], axis=0))
        ins, outs = pair[0:RANK, (k % 2) * TOK : (k % 2 + 1) * TOK], pair[RANK:, (k % 2) * TOK : (k % 2 + 1) * TOK]
        left, right = [], []
        for w in split(outs):
            spread = (w.astype(jnp.float32)[:, None, :] * belongs[None, :, :]).astype(jnp.bfloat16)
            spread = spread.reshape(RANK * 8, TOK)
            left.append(jnp.concatenate([spread[0 : half * 8], spread[half * 8 :]], axis=1))
        for w in split(ins):
            right += [jnp.concatenate([w, nothing], axis=1), jnp.concatenate([nothing, w], axis=1)]
        grads = dot(left[0], jnp.concatenate(right, axis=0), NT)
        grads = grads[:, 0:TOK] + (grads[:, TOK:] + dot(left[1], jnp.concatenate(right[0:2], axis=0), NT))
        gsc[:, k * 8 : (k + 1) * 8, :] = grads.reshape(half, 8, TOK)

    got(qall.at[pl.ds(pl.multiple_of(q_slot(xh, 1 - c), Q_ROWS), Q_ROWS), :], q_recv.at[1])
    got(q_piece(1 - xh, 1 - c, 1 - xl), q_recv.at[3])
    got(q_piece(1 - xh, 1 - c, xl), q_recv.at[4])
    scores = jnp.zeros((2 * 8 * Z, TOK), jnp.float32)
    for m in range(half // 2):
        both = jnp.concatenate([gsc[2 * m], gsc[2 * m + 1]], axis=1)
        hi, lo = split(both)
        scores = scores + dot(jnp.concatenate([hi, lo], axis=0), qall[:, 256 * m : 256 * m + 256], NT)
    sco[...] = scores[0 : 8 * Z] + scores[8 * Z :]
    for d in range(1, Z):
        push(
            sco.at[pl.ds(pl.multiple_of(zp(d) * 8, 8), 8), :], ret.at[d], a_send.at[4, d - 1], a_recv.at[4], z_peer(d)
        )
    ret[0] = sco[pl.ds(pl.multiple_of(z * 8, 8), 8), :]
    got(ret.at[1:Z], a_recv.at[4])
    lane8 = lax.broadcasted_iota(jnp.int32, (8, TOK), 1)
    width = Z * RANK
    for m in range(Z // 2):
        first = ret[zp(-2 * m)]
        second = ret[zp(-2 * m - 1)]
        out_ref[:, 128 * m : 128 * m + 128] = jnp.where(lane8 < RANK, first, pltpu.roll(second, RANK, 1))
        out_ref[:, width + 128 * m : width + 128 * m + 128] = jnp.where(
            lane8 < RANK, pltpu.roll(first, RANK, 1), second
        )
    for copy in pending:
        copy.wait_send()


def solution(mesh):
    Y, Z = mesh.shape["dp"] // 2, mesh.shape["query"] // 4
    H = Z // 2

    def on_device(activations, out_grads, in_projection, out_projection, lengths, queries):
        tokens = activations.shape[0] * mesh.shape["dp"] * mesh.shape["query"]
        f32, bf16 = jnp.float32, jnp.bfloat16
        sem = pltpu.SemaphoreType.DMA
        return pl.pallas_call(
            functools.partial(kernel, Y, Z, tokens),
            out_shape=jax.ShapeDtypeStruct((lengths.shape[0], Z * 4 * Q_ROWS), f32),
            in_specs=[pl.BlockSpec(memory_space=pltpu.HBM)] * 6,
            out_specs=pl.BlockSpec(memory_space=pltpu.VMEM),
            scratch_shapes=[
                pltpu.VMEM((2 * TOK, 2 * Z * IN_PAD), bf16),
                pltpu.VMEM((2 * TOK, out_grads.shape[1]), bf16),
                pltpu.VMEM(in_projection.shape, bf16),
                pltpu.VMEM(out_projection.shape, bf16),
                pltpu.SMEM(lengths.shape, jnp.int32),
                pltpu.VMEM(queries.shape, bf16),
                pltpu.VMEM((RANK, IN_PAD), f32),
                pltpu.VMEM((2 * Z * RANK, BLK), bf16),
                pltpu.VMEM((2, RANK, 2 * TOK), f32),
                pltpu.VMEM((RANK, 2 * TOK), f32),
                pltpu.VMEM((RANK, 2 * TOK), f32),
                pltpu.VMEM((RANK, TOK), f32),
                pltpu.VMEM((2, 8, TOK), f32),
                pltpu.VMEM((4 * Q_ROWS, queries.shape[1]), bf16),
                pltpu.VMEM((Z * TOK, TOK), f32),
                pltpu.VMEM((RANK // 2, TOK), f32),
                pltpu.VMEM((RANK, TOK), f32),
                pltpu.VMEM((3, RANK // 8, TOK), f32),
                pltpu.VMEM((Z - 1, RANK // 8, TOK), f32),
                pltpu.VMEM((Y - 1, RANK // 8, TOK), f32),
                pltpu.VMEM((2, RANK // 8, TOK), f32),
                pltpu.VMEM((RANK // 2, 8 * Z, TOK), f32),
                pltpu.VMEM((8 * Z, TOK), f32),
                pltpu.VMEM((Z, 8, TOK), f32),
                sem((4,)),
                sem((2 * Z,)),
                sem((2 * Z,)),
                sem((2 * Z,)),
                sem((3,)),
                sem((Z,)),
                sem((Z,)),
                sem((2,)),
                sem((2,)),
                sem((Z,)),
                sem((Z,)),
                sem((Z,)),
                sem((Z,)),
                sem((Z,)),
                sem((Z,)),
                sem((6,)),
                sem((2, H, 2)),
                sem((2, H, 2)),
                sem((5,)),
                sem((5,)),
                sem((5, 7)),
                sem((5,)),
            ],
            compiler_params=pltpu.CompilerParams(
                collective_id=0, has_side_effects=True, vmem_limit_bytes=60 * 1024 * 1024
            ),
        )(activations, out_grads, in_projection, out_projection, lengths, queries)

    placed = (
        P(("dp", "query"), None),
        P(("dp", "query"), None),
        P(None, "query"),
        P(None, "query"),
        P(("dp", "query")),
        P("query", None),
    )
    return jax.shard_map(
        on_device, mesh=mesh, in_specs=placed, out_specs=P(("dp", "query"), None), check_vma=False
    )
```

time: 69.7 us -> 63.8 us (0.915)
  Pallas kernels: 67.8 us -> 62.1 us
    pallas_call x1, Pallas kernels: 67.8 us -> 62.1 us  [on_device(): pl.pallas_call(functools.partial(kernel, Y, Z, tokens), out_shape=jax.Sha...]
where the time goes in v3:
time: 63.8 us; the launch traced here: 63.5 us
  Pallas kernels  62.1 us (97%)
  local copies, waits for them, and re-layouts  1.38 us (2%)
    pallas_call x1, Pallas kernels, on_device(): pl.pallas_call(functools.partial(kernel, Y, Z, tokens), out_shape=jax.Sha...  62.1 us
    unnamed x1, local copies, waits for them, and re-layouts  1.38 us

profile of v3, /device:TPU:1, one launch (start us, length us, event | category | flops | bytes accessed | tf_op | source)
XLA Modules:
  0.0 63.5 jit_solution(11657032438037087940)
XLA Ops:
  0.0 62.1 %shard_map.64 = f32[8,1024]{1,0:T(8,128)} custom-call(bf16[128,14336]{1,0:T(8,128)(2,1)} %acts_hbm.1, bf16[128,4096]{1,0:T(8,128)(2,1)} %outg_hbm.1, bf16[64,448]{1,0:T(8,128)(2,1)} %inp_hbm.1, bf16[64,128]{1,0:T(8,128)(2,1)} %outp_hbm.1, s32[8]{0:T(128)} %len_hbm.1, bf16[32,4096]{1,0:T(8,128)(2,1)} %q_hbm.1), custom_call_target="tpu_custom_call" | custom-call | tf_op jit(solution)/shard_map/pallas_call | solution.py:451
  62.1 1.4 %copy.8 = f32[8,1024]{1,0:T(8,128)} copy(f32[8,1024]{1,0:T(8,128)} %shard_map.64) | data formatting | bytes 65536

commit v4 on v3

--- a/solution.py
+++ b/solution.py
@@ -14,7 +14,9 @@
 IN_COLS = 448
 IN_PAD = 512
 OUT_COLS = 128
-BLK = IN_PAD + OUT_COLS
+FULL = 384
+HALF = RANK // 2
+PIECE = 4 * HALF + HALF // 2
 Q_ROWS = 32
 NT = (((1,), (1,)), ((), ()))
 NN = (((1,), (0,)), ((), ()))
@@ -177,20 +179,33 @@
     side = (y + xl) % 2
 
     def piece(h, off, p):
-        return gath.at[pl.ds(pl.multiple_of((h * Z + zp(off)) * RANK + p * 32, 32), 32), :]
+        return gath.at[pl.ds(pl.multiple_of((h * Z + zp(off)) * (2 * PIECE) + p * PIECE, 16), PIECE), :]
 
     def quarter(off, r):
-        return gath.at[pl.ds(pl.multiple_of((xh * Z + zp(off)) * RANK + side * 32 + r * 16, 16), 16), :]
+        first = (xh * Z + zp(off)) * (2 * PIECE) + side * PIECE + r * 80
+        return gath.at[pl.ds(pl.multiple_of(first, 16), PIECE - 80 if r else 80), :]
 
     stage[...] = jnp.zeros_like(stage)
     loads[0].wait()
     loads[1].wait()
     stage[:, 0:IN_COLS] = inp[...].astype(jnp.float32)
     plain = stage[...]
-    shifted = pltpu.roll(plain, IN_PAD - IN_COLS, 1)
-    own_rows = pl.ds(pl.multiple_of((xh * Z + z) * RANK, RANK), RANK)
-    gath[own_rows, 0:IN_PAD] = jnp.where(c == 1, shifted, plain).astype(jnp.bfloat16)
-    gath[own_rows, IN_PAD:BLK] = outp[...]
+    shifted = pltpu.roll(plain, IN_PAD - RANK, 1)
+    full = jnp.where(c == 1, shifted[:, 0:FULL], plain[:, 0:FULL])
+    tile = jnp.where(c == 1, plain[:, 0:128], plain[:, FULL:IN_PAD])
+    lane16 = lax.broadcasted_iota(jnp.int32, (HALF // 2, TOK), 1)
+
+    def block_rows(k, p, first, count):
+        return pl.ds(pl.multiple_of(k * (2 * PIECE) + p * PIECE + first, 16), count)
+
+    for p in range(2):
+        for j in range(3):
+            chunk = full[p * HALF : (p + 1) * HALF, 128 * j : 128 * j + 128]
+            gath[block_rows(xh * Z + z, p, j * HALF, HALF), :] = chunk.astype(jnp.bfloat16)
+        gath[block_rows(xh * Z + z, p, 3 * HALF, HALF), :] = outp[p * HALF : (p + 1) * HALF, :]
+        upper, lower = tile[p * HALF : p * HALF + 16], tile[p * HALF + 16 : (p + 1) * HALF]
+        folded = jnp.where(lane16 < RANK, upper, pltpu.roll(lower, RANK, 1))
+        gath[block_rows(xh * Z + z, p, 4 * HALF, HALF // 2), :] = folded.astype(jnp.bfloat16)
     pl.semaphore_wait(barrier, len(peers))
 
     lane_q = lax.broadcasted_iota(jnp.int32, (Q_ROWS, TOK), 1)
@@ -287,11 +302,22 @@
             k = window(*event)
             own_loads[j].wait()
             got(act_slot(k, 1 - c), act_recv.at[j])
-            rows = pl.ds(pl.multiple_of(k * RANK, RANK), RANK)
-            columns = pl.ds(pl.multiple_of(k * IN_PAD, IN_PAD), IN_PAD)
-            sums[0] = sums[0] + dot(gath[rows, 0:IN_PAD], acts[:, columns], NT)
+            weights = [
+                jnp.concatenate([gath[block_rows(k, p, j * HALF, HALF), :] for p in range(2)], axis=0) for j in range(4)
+            ]
+            last = []
+            for p in range(2):
+                folded = gath[block_rows(k, p, 4 * HALF, HALF // 2), :].astype(jnp.float32)
+                turned = pltpu.roll(folded, RANK, 1)
+                for straight in (0, 1):
+                    last.append(jnp.where(lane16 // RANK == c, jnp.where(c == straight, folded, turned), 0.0))
+            last = jnp.concatenate(last, axis=0).astype(jnp.bfloat16)
+            whole = acts[:, pl.ds(pl.multiple_of(k * IN_PAD + c * 128, 128), FULL)]
+            tile = acts[:, pl.ds(pl.multiple_of(k * IN_PAD + (1 - c) * FULL, 128), 128)]
+            weight = jnp.concatenate(weights[0:3] + [last], axis=1)
+            sums[0] = sums[0] + dot(weight, jnp.concatenate([whole, tile], axis=1), NT)
             columns = pl.ds(pl.multiple_of(k * (2 * OUT_COLS) + c * OUT_COLS, OUT_COLS), OUT_COLS)
-            sums[1] = sums[1] + dot(gath[rows, IN_PAD:BLK], outg[:, columns], NT)
+            sums[1] = sums[1] + dot(weights[3], outg[:, columns], NT)
 
     halves[0] = sums[0]
     halves[1] = sums[1]
@@ -450,7 +476,7 @@
         sem = pltpu.SemaphoreType.DMA
         return pl.pallas_call(
             functools.partial(kernel, Y, Z, tokens),
-            out_shape=jax.ShapeDtypeStruct((lengths.shape[0], Z * 4 * Q_ROWS), f32),
+            out_shape=pltpu.VMEM((lengths.shape[0], Z * 4 * Q_ROWS), f32),
             in_specs=[pl.BlockSpec(memory_space=pltpu.HBM)] * 6,
             out_specs=pl.BlockSpec(memory_space=pltpu.VMEM),
             scratch_shapes=[
@@ -461,7 +487,7 @@
                 pltpu.SMEM(lengths.shape, jnp.int32),
                 pltpu.VMEM(queries.shape, bf16),
                 pltpu.VMEM((RANK, IN_PAD), f32),
-                pltpu.VMEM((2 * Z * RANK, BLK), bf16),
+                pltpu.VMEM((4 * Z * PIECE, TOK), bf16),
                 pltpu.VMEM((2, RANK, 2 * TOK), f32),
                 pltpu.VMEM((RANK, 2 * TOK), f32),
                 pltpu.VMEM((RANK, 2 * TOK), f32),

time: 63.8 us -> 61.8 us (0.969)
  Pallas kernels: 62.1 us -> 60.8 us
  local copies, waits for them, and re-layouts: 1.38 us -> 0.62 us
    pallas_call x1, Pallas kernels: 62.1 us -> 60.8 us  [on_device(): pl.pallas_call(functools.partial(kernel, Y, Z, tokens), out_shape=pltpu.V...]
    unnamed x1, local copies, waits for them, and re-layouts: 1.38 us -> 0.62 us
where the time goes in v4:
time: 61.8 us; the launch traced here: 61.4 us
  Pallas kernels  60.8 us (98%)
  local copies, waits for them, and re-layouts  0.62 us (1%)
    pallas_call x1, Pallas kernels, on_device(): pl.pallas_call(functools.partial(kernel, Y, Z, tokens), out_shape=pltpu.V...  60.8 us

profile of v4, /device:TPU:1, one launch (start us, length us, event | category | flops | bytes accessed | tf_op | source)
XLA Modules:
  0.0 61.4 jit_solution(3417977943623624112)
XLA Ops:
  0.0 60.8 %shard_map.64 = f32[8,1024]{1,0:T(8,128)S(1)} custom-call(bf16[128,14336]{1,0:T(8,128)(2,1)} %acts_hbm.1, bf16[128,4096]{1,0:T(8,128)(2,1)} %outg_hbm.1, bf16[64,448]{1,0:T(8,128)(2,1)} %inp_hbm.1, bf16[64,128]{1,0:T(8,128)(2,1)} %outp_hbm.1, s32[8]{0:T(128)} %len_hbm.1, bf16[32,4096]{1,0:T(8,128)(2,1)} %q_hbm.1), custom_call_target="tpu_custom_call" | custom-call | tf_op jit(solution)/shard_map/pallas_call | solution.py:477
  60.8 0.6 %copy.8 = f32[8,1024]{1,0:T(8,128)} copy(f32[8,1024]{1,0:T(8,128)S(1)} %shard_map.64) | data formatting | bytes 65536

commit v5 on v4

--- a/solution.py
+++ b/solution.py
@@ -97,6 +97,11 @@
     return [event[1:] for event in sorted(order, key=lambda event: event[0])]
 
 
+def far_first(count):
+    half = count // 2
+    return [half] + [sign * d for d in range(half - 1, 0, -1) for sign in (1, -1)] + [0]
+
+
 def goes_on(H, dist, way, part):
     return dist + 1 < H or (dist + 1 == H and part == way)
 
@@ -145,6 +150,10 @@
 
     def got(ref, sem):
         pltpu.make_async_copy(ref, ref, sem).wait()
+
+    def settle(keep):
+        while len(pending) > keep:
+            pending.pop(0).wait_send()
 
     loads = [
         pltpu.make_async_copy(inp_hbm, inp, loc_sem.at[0]),
@@ -366,24 +375,27 @@
             spare[...] = both[:, (1 - cc) * TOK : (2 - cc) * TOK]
 
     push(spare, tok_piece(z, c), sw_sem.at[4], sw_sem.at[5], sibling)
+    settle(30)
     got(ar1, a_recv.at[0])
     summed = part[x_rows(0), :]
     for j in range(3):
         summed = summed + ar1[j]
     mine[0] = summed
-    for d in range(1, Z):
+    for d in [off % Z for off in far_first(Z)[:-1]]:
         push(mine.at[0], ar2.at[d - 1], a_send.at[1, d - 1], a_recv.at[1], z_peer(d))
     got(tok_piece(z, 1 - c), sw_sem.at[5])
     tok_step(0)
+    settle(25)
     tok_step(1)
     got(ar2, a_recv.at[1])
     for d in range(Z - 1):
         summed = summed + ar2[d]
     mine[1] = summed
-    for d in range(1, Y):
+    for d in [off % Y for off in far_first(Y)[:-1]]:
         push(mine.at[1], ar3.at[d - 1], a_send.at[2, d - 1], a_recv.at[2], y_peer(d))
     if H > 2:
         tok_step(2)
+    settle(25)
     got(ar3, a_recv.at[2])
     for d in range(Y - 1):
         summed = summed + ar3[d]
@@ -397,6 +409,7 @@
         push(here, here, a_send.at[3, m - 1], a_recv.at[3], x_peer(m))
     if H > 3:
         tok_step(3)
+    settle(15)
     got(total.at[0 : RANK - rows_x, :], a_recv.at[3])
     if H > 1:
         tok_step(H)
@@ -420,9 +433,16 @@
     token = lax.broadcasted_iota(jnp.int32, (SEQ // 2, TOK), 1)
     belongs = (token // SEQ == example).astype(jnp.float32)
     nothing = jnp.zeros((RANK, TOK), jnp.bfloat16)
+    got(qall.at[pl.ds(pl.multiple_of(q_slot(xh, 1 - c), Q_ROWS), Q_ROWS), :], q_recv.at[1])
+    got(q_piece(1 - xh, 1 - c, 1 - xl), q_recv.at[3])
+    got(q_piece(1 - xh, 1 - c, xl), q_recv.at[4])
+    offs = far_first(Z)
+    group = Z // 2
     for k in range(Z):
         if k % 2 == 0:
-            rows = [split(tok[(k + i) * TOK : (k + i + 1) * TOK, :]) for i in range(2)]
+            rows = [
+                split(tok[pl.ds(pl.multiple_of(zp(off) * TOK, TOK), TOK), :]) for off in offs[k : k + 2]
+            ]
             hi = jnp.concatenate([rows[0][0], rows[1][0]], axis=1)
             lo = jnp.concatenate([rows[0][1], rows[1][1]], axis=1)
             pair = dot(blocks, jnp.concatenate([hi, hi, lo], axis=0))
@@ -437,21 +457,22 @@
         grads = dot(left[0], jnp.concatenate(right, axis=0), NT)
         grads = grads[:, 0:TOK] + (grads[:, TOK:] + dot(left[1], jnp.concatenate(right[0:2], axis=0), NT))
         gsc[:, k * 8 : (k + 1) * 8, :] = grads.reshape(half, 8, TOK)
-
-    got(qall.at[pl.ds(pl.multiple_of(q_slot(xh, 1 - c), Q_ROWS), Q_ROWS), :], q_recv.at[1])
-    got(q_piece(1 - xh, 1 - c, 1 - xl), q_recv.at[3])
-    got(q_piece(1 - xh, 1 - c, xl), q_recv.at[4])
-    scores = jnp.zeros((2 * 8 * Z, TOK), jnp.float32)
-    for m in range(half // 2):
-        both = jnp.concatenate([gsc[2 * m], gsc[2 * m + 1]], axis=1)
-        hi, lo = split(both)
-        scores = scores + dot(jnp.concatenate([hi, lo], axis=0), qall[:, 256 * m : 256 * m + 256], NT)
-    sco[...] = scores[0 : 8 * Z] + scores[8 * Z :]
-    for d in range(1, Z):
-        push(
-            sco.at[pl.ds(pl.multiple_of(zp(d) * 8, 8), 8), :], ret.at[d], a_send.at[4, d - 1], a_recv.at[4], z_peer(d)
-        )
-    ret[0] = sco[pl.ds(pl.multiple_of(z * 8, 8), 8), :]
+        if (k + 1) % group:
+            continue
+        first = k + 1 - group
+        scores = jnp.zeros((2 * 8 * group, TOK), jnp.float32)
+        for m in range(half // 2):
+            mine_both = [gsc[2 * m + i, first * 8 : (k + 1) * 8, :] for i in range(2)]
+            hi, lo = split(jnp.concatenate(mine_both, axis=1))
+            scores = scores + dot(jnp.concatenate([hi, lo], axis=0), qall[:, 256 * m : 256 * m + 256], NT)
+        sco[first * 8 : (k + 1) * 8, :] = scores[0 : 8 * group] + scores[8 * group :]
+        for j in range(first, k + 1):
+            if offs[j] == 0:
+                ret[0] = sco[j * 8 : (j + 1) * 8, :]
+            else:
+                d = offs[j] % Z
+                push(sco.at[j * 8 : (j + 1) * 8, :], ret.at[d], a_send.at[4, d - 1], a_recv.at[4], z_peer(d))
+    settle(Z // 2 - 1)
     got(ret.at[1:Z], a_recv.at[4])
     lane8 = lax.broadcasted_iota(jnp.int32, (8, TOK), 1)
     width = Z * RANK
@@ -462,8 +483,7 @@
         out_ref[:, width + 128 * m : width + 128 * m + 128] = jnp.where(
             lane8 < RANK, pltpu.roll(first, RANK, 1), second
         )
-    for copy in pending:
-        copy.wait_send()
+    settle(0)
 
 
 def solution(mesh):

time: 61.8 us -> 61 us (0.987)
  Pallas kernels: 60.8 us -> 59.4 us
    pallas_call x1, Pallas kernels: 60.8 us -> 59.4 us  [on_device(): pl.pallas_call(functools.partial(kernel, Y, Z, tokens), out_shape=pltpu.V...]
where the time goes in v5:
time: 61 us; the launch traced here: 60 us
  Pallas kernels  59.4 us (97%)
  local copies, waits for them, and re-layouts  0.62 us (1%)
    pallas_call x1, Pallas kernels, on_device(): pl.pallas_call(functools.partial(kernel, Y, Z, tokens), out_shape=pltpu.V...  59.4 us

profile of v5, /device:TPU:1, one launch (start us, length us, event | category | flops | bytes accessed | tf_op | source)
XLA Modules:
  0.0 60.0 jit_solution(16585629988888134661)
XLA Ops:
  0.0 59.4 %shard_map.64 = f32[8,1024]{1,0:T(8,128)S(1)} custom-call(bf16[128,14336]{1,0:T(8,128)(2,1)} %acts_hbm.1, bf16[128,4096]{1,0:T(8,128)(2,1)} %outg_hbm.1, bf16[64,448]{1,0:T(8,128)(2,1)} %inp_hbm.1, bf16[64,128]{1,0:T(8,128)(2,1)} %outp_hbm.1, s32[8]{0:T(128)} %len_hbm.1, bf16[32,4096]{1,0:T(8,128)(2,1)} %q_hbm.1), custom_call_target="tpu_custom_call" | custom-call | tf_op jit(solution)/shard_map/pallas_call | solution.py:497
  59.4 0.6 %copy.8 = f32[8,1024]{1,0:T(8,128)} copy(f32[8,1024]{1,0:T(8,128)S(1)} %shard_map.64) | data formatting | bytes 65536

commit v6 on v5

--- a/solution.py
+++ b/solution.py
@@ -375,6 +375,8 @@
             spare[...] = both[:, (1 - cc) * TOK : (2 - cc) * TOK]
 
     push(spare, tok_piece(z, c), sw_sem.at[4], sw_sem.at[5], sibling)
+    got(tok_piece(z, 1 - c), sw_sem.at[5])
+    tok_step(0)
     settle(30)
     got(ar1, a_recv.at[0])
     summed = part[x_rows(0), :]
@@ -383,8 +385,6 @@
     mine[0] = summed
     for d in [off % Z for off in far_first(Z)[:-1]]:
         push(mine.at[0], ar2.at[d - 1], a_send.at[1, d - 1], a_recv.at[1], z_peer(d))
-    got(tok_piece(z, 1 - c), sw_sem.at[5])
-    tok_step(0)
     settle(25)
     tok_step(1)
     got(ar2, a_recv.at[1])

time: 61 us -> 60.2 us (0.987); the launches traced: 60 us -> 60.1 us
  no operation moved by 1% of the time
where the time goes in v6:
time: 60.2 us; the launch traced here: 60.1 us
  Pallas kernels  59.5 us (99%)
  local copies, waits for them, and re-layouts  0.62 us (1%)
    pallas_call x1, Pallas kernels, on_device(): pl.pallas_call(functools.partial(kernel, Y, Z, tokens), out_shape=pltpu.V...  59.5 us

profile of v6, /device:TPU:1, one launch (start us, length us, event | category | flops | bytes accessed | tf_op | source)
XLA Modules:
  0.0 60.1 jit_solution(7510203352198537291)
XLA Ops:
  0.0 59.5 %shard_map.64 = f32[8,1024]{1,0:T(8,128)S(1)} custom-call(bf16[128,14336]{1,0:T(8,128)(2,1)} %acts_hbm.1, bf16[128,4096]{1,0:T(8,128)(2,1)} %outg_hbm.1, bf16[64,448]{1,0:T(8,128)(2,1)} %inp_hbm.1, bf16[64,128]{1,0:T(8,128)(2,1)} %outp_hbm.1, s32[8]{0:T(128)} %len_hbm.1, bf16[32,4096]{1,0:T(8,128)(2,1)} %q_hbm.1), custom_call_target="tpu_custom_call" | custom-call | tf_op jit(solution)/shard_map/pallas_call | solution.py:497
  59.5 0.6 %copy.8 = f32[8,1024]{1,0:T(8,128)} copy(f32[8,1024]{1,0:T(8,128)S(1)} %shard_map.64) | data formatting | bytes 65536
